TPU v7x, 32 devices: a whole 2x2x4 slice. The times are simulated.
32 devices in a mesh: dp: 4 (over y, x), expert: 8 (over z, core).
Axes of the slice: x: 2, y: 2, z: 4, core: 2. Of those that a mesh axis runs over, the one named last changes fastest.
Arguments:
- hidden_in: bfloat16 [4096, 2880], P(('dp', 'expert')), may hold values from -6 to 6
- queries: bfloat16 [4096, 4096], P(('dp', 'expert')), may hold values from -50 to 50
- kv_pages: bfloat16 [512, 128, 1024], P(('dp', 'expert')), may hold values from -4.5 to 4.5
- page_table: int32 [128, 4], P(('dp', 'expert')), may hold values from 0 to 15, as said below
- new_rows: int32 [128], P(('dp', 'expert')), may hold values from 1 to 125, as said below
- context: int32 [128], P(('dp', 'expert')), may hold values from 1 to 512, as said below
- sink_logits: float32 [64], replicated, may hold values from 0 to 8
- out_proj: bfloat16 [4096, 2880], P('dp'), may hold values from -0.09375 to 0.09375
- norm_gain: float32 [2880], replicated, may hold values from 0.1 to 1.9
- routes: int32 [4096, 4], P(('dp', 'expert')), may hold values from 0 to 31, all different within a row; in each aligned block of 128 rows (0 to 127, 128 to 255, ...) at most 20 rows name the same one
- route_weights: float32 [4096, 4], P(('dp', 'expert')), may hold values from 0.05 to 1
- gate_up: bfloat16 [32, 2, 2880, 2048], P('expert', None, None, 'dp'), may hold values from -0.109375 to 0.109375
- down_proj: bfloat16 [32, 2048, 2880], P('expert', 'dp'), may hold values from -0.125 to 0.125
Outputs:
- layer_out: bfloat16 [4096, 2880], P(('dp', 'expert'))
Inputs may be any that keep to these rules, and one draw needn't show every extreme that they name: `page_table`: each request's table row lists distinct pages of its own block of 16 pages; each block's table holds each of its page numbers once. The new_rows of one block of 4 requests sum to 128; one to three requests of each block have more than one. new_rows <= context; in every block some request has context 4 * 128. Within the 128 rows of one block, no expert is named by more than 20 routes; some expert reaches 20 in every draw.
All inputs are finite; a program needn't handle non-finite values.
Results may differ from a plain program's by a relative error of at most 0.015.
Values may be sent and summed in bfloat16 or wider, within the bound.
No kernel may reach another device: no remote copies, remote signals or barrier semaphores. Data moves between devices by JAX's collectives and lax.ppermute only.
A program may use at most 128 MiB of HBM per device.

v0:
```python
import math

import jax
import jax.numpy as jnp
from jax import lax
from jax.sharding import PartitionSpec as P

QH = 64
KVH = 8
HD = 64
E = 32
CAP = 20


norm_eps = 1e-05


def attend_rows(queries, kv_pages, page_table, new_rows, context, sink_logits):
    row_count = queries.shape[0]
    req_count = new_rows.shape[0]
    page_count = kv_pages.shape[0]
    page_len = kv_pages.shape[1]
    per_req = page_table.shape[1]
    req_ends = jnp.cumsum(new_rows)
    row_index = jnp.arange(row_count, dtype=jnp.int32)
    owner_req = jnp.sum((row_index[:, None] >= req_ends[None, :]).astype(jnp.int32), axis=1)
    pick_req = (owner_req[:, None] == jnp.arange(req_count, dtype=jnp.int32)[None, :]).astype(
        jnp.int32
    )
    position = row_index + jnp.sum(pick_req * (context - req_ends)[None, :], axis=1)
    match = (
        page_table[:, :, None] == jnp.arange(page_count, dtype=jnp.int32)[None, None, :]
    ).astype(jnp.int32)
    order_in_req = (
        jnp.sum(match * (jnp.arange(per_req, dtype=jnp.int32) + 1)[None, :, None], axis=1) - 1
    )
    row_page_pos = jnp.sum(pick_req[:, :, None] * order_in_req[None, :, :], axis=1)
    offsets = jnp.arange(page_len, dtype=jnp.int32)
    slot_pos = row_page_pos[:, :, None] * page_len + offsets[None, None, :]
    visible = (row_page_pos[:, :, None] >= 0) & (slot_pos <= position[:, None, None])
    visible = visible.reshape(row_count, page_count * page_len)
    flat_cache = kv_pages.reshape(page_count * page_len, kv_pages.shape[2])
    group_size = QH // KVH

    def one_head(head_idx):
        kv_head = lax.dynamic_slice_in_dim(flat_cache, head_idx * 2 * HD, 2 * HD, 1)
        key_part = kv_head[:, :HD]
        value_part = kv_head[:, HD:]
        query_part = lax.dynamic_slice_in_dim(
            queries, head_idx * group_size * HD, group_size * HD, 1
        )
        query_part = query_part.reshape(row_count, group_size, HD)
        sink_part = lax.dynamic_slice_in_dim(sink_logits, head_idx * group_size, group_size, 0)
        scores = jnp.einsum(
            "rgd,sd->rgs", query_part, key_part, preferred_element_type=jnp.float32
        ) * (1.0 / math.sqrt(HD))
        scores = jnp.where(visible[:, None, :], scores, -jnp.inf)
        row_max = jnp.maximum(jnp.max(scores, axis=2), sink_part[None, :])
        weight = jnp.exp(scores - row_max[:, :, None])
        denom_sum = jnp.sum(weight, axis=2) + jnp.exp(sink_part[None, :] - row_max)
        probs_bf = (weight / denom_sum[:, :, None]).astype(jnp.bfloat16)
        return jnp.einsum(
            "rgs,sd->rgd", probs_bf, value_part, preferred_element_type=jnp.float32
        ).astype(jnp.bfloat16)

    head_parts = lax.map(one_head, jnp.arange(KVH, dtype=jnp.int32))
    return jnp.transpose(head_parts, (1, 0, 2, 3)).reshape(row_count, QH * HD)


def expert_terms(gathered_rows, gate_up, down_proj):
    local_count = gate_up.shape[0]
    senders = gathered_rows.shape[0] // local_count
    blocks = gathered_rows.reshape(
        senders, local_count, gathered_rows.shape[1], gathered_rows.shape[2]
    )
    gate_up_f = jnp.einsum("sjcd,jtdf->sjctf", blocks, gate_up, preferred_element_type=jnp.float32)
    gate_f = gate_up_f[:, :, :, 0, :]
    up_f = gate_up_f[:, :, :, 1, :]
    hidden = ((up_f + 1.0) * gate_f * jax.nn.sigmoid(1.702 * gate_f)).astype(jnp.bfloat16)
    down_f = jnp.einsum("sjcf,jfd->sjcd", hidden, down_proj, preferred_element_type=jnp.float32)
    return down_f.reshape(gathered_rows.shape)


def per_device(
    hidden_in,
    queries,
    kv_pages,
    page_table,
    new_rows,
    context,
    sink_logits,
    out_proj,
    norm_gain,
    routes,
    route_weights,
    gate_up,
    down_proj,
):
    row_count = hidden_in.shape[0]
    model_width = hidden_in.shape[1]
    attended = attend_rows(queries, kv_pages, page_table, new_rows, context, sink_logits)
    head_parts = lax.all_to_all(attended, "dp", split_axis=1, concat_axis=0, tiled=True)
    o_out = lax.psum_scatter(
        jnp.dot(head_parts, out_proj, preferred_element_type=jnp.float32).astype(jnp.bfloat16),
        "dp",
        scatter_dimension=0,
        tiled=True,
    ).astype(jnp.float32)
    mixed = (hidden_in.astype(jnp.float32) + o_out).astype(jnp.bfloat16)
    mixed_f = mixed.astype(jnp.float32)
    normed = (
        mixed_f
        * lax.rsqrt(jnp.mean(mixed_f * mixed_f, axis=1, keepdims=True) + norm_eps)
        * norm_gain
    ).astype(jnp.bfloat16)
    assign = routes.reshape(-1)
    onehot = (assign[:, None] == jnp.arange(E, dtype=jnp.int32)[None, :]).astype(jnp.int32)
    slot_index = jnp.sum((jnp.cumsum(onehot, axis=0) - onehot) * onehot, axis=1)
    source = jnp.arange(assign.shape[0], dtype=jnp.int32) // routes.shape[1]
    send_rows = (
        jnp.zeros((E, CAP, model_width), jnp.bfloat16).at[assign, slot_index].set(normed[source])
    )
    dp_count = lax.axis_size("dp")
    copies = jnp.broadcast_to(send_rows[None], (dp_count,) + send_rows.shape).reshape(
        dp_count * E, CAP, model_width
    )
    gathered_rows = lax.all_to_all(
        copies, ("dp", "expert"), split_axis=0, concat_axis=0, tiled=True
    )
    partials = expert_terms(gathered_rows, gate_up, down_proj).astype(jnp.bfloat16)
    returned_parts = lax.all_to_all(
        partials, ("dp", "expert"), split_axis=0, concat_axis=0, tiled=True
    )
    returned = jnp.sum(
        returned_parts.reshape(dp_count, E, CAP, model_width).astype(jnp.float32), axis=0
    )
    picked = returned[assign, slot_index]
    expert_mix = jnp.sum(
        (picked * route_weights.reshape(-1)[:, None]).reshape(
            row_count, routes.shape[1], model_width
        ),
        axis=1,
    )
    return (mixed_f + expert_mix).astype(jnp.bfloat16)


def solution(mesh):
    return jax.shard_map(
        per_device,
        mesh=mesh,
        in_specs=(
            P(("dp", "expert"), None),
            P(("dp", "expert"), None),
            P(("dp", "expert"), None, None),
            P(("dp", "expert"), None),
            P(("dp", "expert")),
            P(("dp", "expert")),
            P(),
            P("dp", None),
            P(),
            P(("dp", "expert"), None),
            P(("dp", "expert"), None),
            P("expert", None, None, "dp"),
            P("expert", "dp", None),
        ),
        out_specs=P(("dp", "expert"), None),
        check_vma=False,
    )
```

profile of v0, /device:TPU:0, one launch (start us, length us, event | category | flops | bytes accessed | tf_op | source)
XLA Modules:
  0.0 1289.0 jit_solution(2493678325523130642)
XLA Ops:
  9.3 172.1 %while.13 = (s32[]{:T(128)}, bf16[8,128,8,64]{1,3,2,0:T(8,128)(2,1)S(1)}, s32[8]{0:T(128)S(1)}, bf16[128,4096]{1,0:T(8,128)(2,1)}, bf16[2048,1024]{1,0:T(8,128)(...) while((s32[]{:T(128)}, ...), condition=%wide.region_8.9_spmd.clone, body=%wide.region_5.8_spmd.clone.sunk | while | flops 562890752 | bytes 28627444 | solution.py:66
  13.6 5.9 fusion.55
  20.4 4.5 fusion.56
  25.0 5.8 fusion.57
  35.1 5.9 fusion.55
  41.9 4.5 fusion.56
  46.5 5.8 fusion.57
  56.7 5.9 fusion.55
  63.4 4.5 fusion.56
  68.0 5.8 fusion.57
  78.2 5.9 fusion.55
  84.9 4.5 fusion.56
  89.5 5.8 fusion.57
  99.7 5.9 fusion.55
  106.4 4.5 fusion.56
  111.0 5.8 fusion.57
  121.2 5.9 fusion.55
  127.9 4.5 fusion.56
  132.5 5.8 fusion.57
  142.7 5.9 fusion.55
  149.4 4.5 fusion.56
  154.1 5.8 fusion.57
  164.2 5.9 fusion.55
  171.0 4.5 fusion.56
  175.6 5.8 fusion.57
  181.4 19.1 %all_to_all.29 = bf16[128,4,1024]{0,2,1:T(8,128)(2,1)S(1)} all-to-all(bf16[128,4,1024]{0,2,1:T(8,128)(2,1)S(1)} %bitcast.118), channel_id=1, replica_groups=mesh['dp'=4,'expert'=8] {'dp'}, dimensions={1} | all-to-all | bytes 2097152 | tf_op jit(solution)/shard_map/all_to_all | solution.py:102
  201.1 7.3 convolution_convert_fusion
  208.4 4.6 copy.119
  215.7 40.1 %reduce-scatter.4.cloned.1.call-done = bf16[128,2880]{1,0:T(8,128)(2,1)} async-done(((bf16[512,2880]{1,0:T(8,128)(2,1)}), bf16[128,2880]{1,0:T(8,128)(2,1)}) %reduce-scatter.4.cloned.1.call-update) | async-done | bytes 737296
  255.8 1.5 copy.120
  259.0 3.8 gather_fusion
  262.7 2.1 broadcast_in_dim.41
  264.8 111.6 %scatter_fusion = bf16[32,20,2880]{2,0,1:T(8,128)(2,1)} fusion(bf16[32,20,2880]{2,0,1:T(8,128)(2,1)} %broadcast_in_dim.41, s32[512]{0:T(512)S(1)} %bitcast.111, bf16[512,2880]{1,0:T(8,128)(2,1)} %gather_fusion), kind=kCustom, calls=%fused_computation.2 | custom fusion | bytes 8851456 | tf_op jit(solution)/shard_map/scatter | solution.py:121
  376.4 3.2 copy.102
  379.6 1.5 broadcast_in_dim.42
  381.1 397.4 %all_to_all.30 = bf16[128,20,2880]{2,1,0:T(8,128)(2,1)} all-to-all(bf16[128,20,2880]{2,1,0:T(8,128)(2,1)S(1)} %bitcast.106), channel_id=1, replica_groups=mesh['dp'=4,'expert'=8] {'dp','expert'}, dimensions={0} | all-to-all | bytes 29491200 | tf_op jit(solution)/shard_map/all_to_all | solution.py:127
  778.5 25.8 %fusion.24 = f32[32,4,20,2,512]{4,0,3,2,1:T(8,128)} fusion(bf16[4,2,2880,512]{3,2,1,0:T(8,128)(2,1)} %param.26, bf16[32,4,20,2880,1]{3,2,1,0,4:T(8,128)(2,1)} %bitcast.114), kind=kOutput, calls=%fused_computation.39 | convolution fusion | flops 15099494400 | bytes 48824320 | tf_op jit(solution)/shard_map/sjcd,jtdf->sjctf/dot_general | solution.py:76
  804.4 17.2 %convert_bitcast_fusion = bf16[32,4,20,2880]{3,0,2,1:T(8,128)(2,1)} fusion(bf16[4,512,2880]{1,2,0:T(8,128)(2,1)} %param.27, f32[32,4,20,2,512]{4,0,3,2,1:T(8,128)} %fusion.24), kind=kOutput, calls=%fused_computation.30 | convolution fusion | flops 7567605760 | bytes 37027840 | tf_op jit(solution)/shard_map/sjcf,jfd->sjcd/dot_general | solution.py:80
  821.6 15.2 %copy.118 = bf16[32,4,20,2880]{3,2,1,0:T(8,128)(2,1)} copy(bf16[32,4,20,2880]{3,0,2,1:T(8,128)(2,1)} %convert_bitcast_fusion) | data formatting | bytes 29491200 | tf_op jit(solution)/shard_map/convert_element_type | solution.py:130
  836.8 4.3 all-to-all-start.2
  841.3 392.4 %all-to-all-done.2 = bf16[128,20,2880]{2,1,0:T(8,128)(2,1)} async-done(((bf16[128,20,2880]{2,1,0:T(8,128)(2,1)}), bf16[128,20,2880]{2,1,0:T(8,128)(2,1)}, u32[]{:S(2)}, u32[]{:S(2)}) %all-to-all-start.2) | async-done | bytes 14745632 | tf_op jit(solution)/shard_map/all_to_all | solution.py:131
  1233.7 10.2 convert_reduce_fusion
  1243.9 4.4 copy.107
  1248.2 15.1 %gather_fusion.1 = f32[512,2880]{1,0:T(8,128)} fusion(f32[32,20,2880]{2,0,1:T(8,128)} %copy.107, s32[512]{0:T(512)S(1)} %bitcast.112), kind=kCustom, calls=%fused_computation.1 | custom fusion | bytes 11800576 | tf_op jit(solution)/shard_map/gather | solution.py:137
  1263.3 7.6 gather.10
  1271.0 7.1 multiply_reduce_fusion
  1278.0 1.6 copy.109
  1279.6 2.5 fusion.35
  (133 shorter events, 32.4 us)
Async XLA Ops:
  6.5 249.3 %reduce-scatter.4.cloned.1.call-start = ((), (), s32[]{:S(2)}) async-start(), calls=%async_computation.4 | async-start | bytes 3768320
  9.3 10.9 copy-start.8
  30.8 10.9 copy-start.8
  52.4 10.9 copy-start.8
  73.9 10.9 copy-start.8
  95.4 10.9 copy-start.8
  116.9 10.9 copy-start.8
  138.4 10.9 copy-start.8
  159.9 10.9 copy-start.8
  208.4 4.7 copy-start.6
  208.4 48.9 %copy-start.3 = (bf16[128,2880]{0,1:T(8,128)(2,1)S(1)}, bf16[128,2880]{0,1:T(8,128)(2,1)}, u32[]{:S(2)}) copy-start(bf16[128,2880]{0,1:T(8,128)(2,1)} %param.15) | copy-start | bytes 2211844
  208.4 49.8 %copy-start.5 = (f32[2880]{0:T(1024)S(1)}, f32[2880]{0:T(1024)}, u32[]{:S(2)}) copy-start(f32[2880]{0:T(1024)} %param.23) | copy-start | bytes 34564
  257.3 0.9 copy-start.1
  836.8 4.3 copy-start.7
  836.8 396.9 %all-to-all-start.2 = ((bf16[128,20,2880]{2,1,0:T(8,128)(2,1)}), bf16[128,20,2880]{2,1,0:T(8,128)(2,1)}, u32[]{:S(2)}, u32[]{:S(2)}) async-start(bf16[128,20,2880]{2,1,0:T(8,128)(2,1)} %bitcast.107), calls=%async_computation.2 | async-start | bytes 36175872 | tf_op jit(solution)/shard_map/all_to_all | solution.py:131
  1243.9 4.4 copy-start
  1270.9 8.7 copy-start.2
  1271.0 8.7 copy-start.4
Sparse Core Ops, SparseCore 0:
  213.2 42.5 reduce-scatter.3
where the time goes:
time: 1290 us
  waiting for transfers between devices  432 us (33%)
  blocking collectives  417 us (32%)
  local copies, waits for them, and re-layouts  190 us (15%)
  matrix products  144 us (11%)
  other arithmetic  70.6 us (5%)
  loops' own time  17.4 us (1%)
  between operations  13.6 us (1%)
    all_to_all x1, blocking collectives, per_device(): lax.all_to_all(copies, ('dp', 'expert'), split_axis=0, concat_axis=0, til...  397 us
    all_to_all x1, waiting for transfers between devices, per_device(): lax.all_to_all(partials, ('dp', 'expert'), split_axis=0, concat_axis=0, t...  392 us
    scatter x2, local copies, waits for them, and re-layouts, per_device(): jnp.zeros((E, CAP, model_width), jnp.bfloat16).at[assign, slot_index]  115 us
    dot_general x8, matrix products, one_head(): jnp.einsum('rgd,sd->rgs', query_part, key_part, preferred_element_type=jn...  47 us
    dot_general x8, matrix products, one_head(): jnp.einsum('rgs,sd->rgd', probs_bf, value_part, preferred_element_type=jn...  46.8 us
    unnamed x2, waiting for transfers between devices  40.1 us
    reduce_sum x8, other arithmetic, one_head(): denom_sum = jnp.sum(weight, axis=2) + jnp.exp(sink_part[None, :] - row_max)  36.3 us
    dot_general x1, matrix products, expert_terms(): jnp.einsum('sjcd,jtdf->sjctf', blocks, gate_up, preferred_element_type=jn...  25.8 us
  transfers between devices with their start and end apart: 2, of which 2 were waited for; matrix products, arithmetic and copies ran while one was open for 0% of the time, Pallas kernels for 0%

commit v1 on v0

v1 whole, which is shorter than its diff:
```python
import functools

import jax
import jax.numpy as jnp
from jax import lax
from jax.experimental import pallas as pl
from jax.experimental.pallas import tpu as pltpu
from jax.sharding import Mesh
from jax.sharding import PartitionSpec as P

QH = 64
KVH = 8
HD = 64
E = 32
CAP = 20
GROUP = QH // KVH
TILE = 32
PACK = 4

norm_eps = 1e-05
F32 = jnp.float32
BF16 = jnp.bfloat16


def params(mib, **kw):
    return pltpu.CompilerParams(vmem_limit_bytes=mib << 20, **kw)


def attend_kernel(
    col_s, rows_s, ctx_s, table_s, sink_s, q_ref, kv_ref, o_ref, *, kv_heads, reqs, per_req
):
    page_len = kv_ref.shape[1]
    span = per_req * page_len
    width = 2 * HD
    lane = lax.broadcasted_iota(jnp.int32, (1, width), 1)
    low = lane < HD
    slot = lax.broadcasted_iota(jnp.int32, (1, span), 1)
    row_in = lax.broadcasted_iota(jnp.int32, (TILE, 1), 0)
    head0 = col_s[0] * kv_heads * GROUP

    def one_tile(req, first, last, tile):
        r0 = pl.multiple_of(tile * TILE, TILE)
        row = row_in + r0
        mine = (row >= first) & (row < last)
        limit = jnp.where(mine, row + (ctx_s[req] - last), -1)
        limit = jnp.concatenate([limit] * GROUP, axis=0)
        seen = slot <= limit
        for k in range(kv_heads):
            kv = jnp.concatenate(
                [
                    kv_ref[table_s[req * per_req + p], :, k * width : (k + 1) * width]
                    for p in range(per_req)
                ],
                axis=0,
            )
            parts, sinks = [], []
            for g in range(0, GROUP, 2):
                c0 = (k * GROUP + g) * HD
                pair = q_ref[pl.ds(r0, TILE), c0 : c0 + width].astype(F32) * (HD**-0.5)
                parts.append(jnp.where(low, pair, 0.0).astype(BF16))
                parts.append(jnp.where(low, pltpu.roll(pair, HD, 1), 0.0).astype(BF16))
                for h in (g, g + 1):
                    sinks.append(jnp.full((TILE, 1), sink_s[head0 + k * GROUP + h], F32))
            q = jnp.concatenate(parts, axis=0)
            sink = jnp.concatenate(sinks, axis=0)
            score = lax.dot_general(q, kv, (((1,), (1,)), ((), ())), preferred_element_type=F32)
            score = jnp.where(seen, score, -jnp.inf)
            top = jnp.maximum(jnp.max(score, axis=1, keepdims=True), sink)
            prob = jnp.exp(score - top).astype(BF16)
            ones_v = jnp.where(low, jnp.ones_like(kv), kv)
            both = jnp.dot(prob, ones_v, preferred_element_type=F32)
            swapped = pltpu.roll(both, HD, 1)
            norm = jnp.where(low, both, swapped) + jnp.exp(sink - top)
            out = jnp.where(low, swapped, both) / norm
            for g in range(0, GROUP, 2):
                a = out[g * TILE : (g + 1) * TILE]
                b = out[(g + 1) * TILE : (g + 2) * TILE]
                c0 = (k * GROUP + g) * HD
                old = o_ref[pl.ds(r0, TILE), c0 : c0 + width]
                new = jnp.where(low, a, b).astype(BF16)
                o_ref[pl.ds(r0, TILE), c0 : c0 + width] = jnp.where(mine, new, old)

    def one_req(req, first):
        last = first + rows_s[req]

        def step(tile, carry):
            one_tile(req, first, last, tile)
            return carry

        lax.fori_loop(first // TILE, (last - 1) // TILE + 1, step, 0)
        return last

    lax.fori_loop(0, reqs, one_req, jnp.int32(0))


def attend_group(col, queries, kv_pages, page_table, new_rows, context, sink_logits, groups):
    rows = queries.shape[0]
    pages, page_len, kv_width = kv_pages.shape
    reqs, per_req = page_table.shape
    kv_heads = KVH // groups
    q_width = queries.shape[1] // groups
    body = functools.partial(attend_kernel, kv_heads=kv_heads, reqs=reqs, per_req=per_req)
    flops = 2 * 2 * rows * q_width * per_req * page_len
    return pl.pallas_call(
        body,
        grid_spec=pltpu.PrefetchScalarGridSpec(
            num_scalar_prefetch=5,
            grid=(1,),
            in_specs=[
                pl.BlockSpec((rows, q_width), lambda i, col, *_: (0, col[0])),
                pl.BlockSpec(
                    (pages, page_len, kv_width // groups), lambda i, col, *_: (0, 0, col[0])
                ),
            ],
            out_specs=pl.BlockSpec((rows, q_width), lambda i, *_: (0, 0)),
        ),
        out_shape=jax.ShapeDtypeStruct((rows, q_width), BF16),
        compiler_params=params(32),
        cost_estimate=pl.CostEstimate(
            flops=8 * flops,
            bytes_accessed=2 * (2 * rows * q_width + pages * page_len * kv_width // groups),
            transcendentals=0,
        ),
        name="attend",
    )(col, new_rows, context, page_table.reshape(-1), sink_logits, queries, kv_pages)


def mix_kernel(x_ref, a_ref, b_ref, c_ref, d_ref, gain_ref, mixed_ref, normed_ref):
    total = a_ref[...].astype(F32) + b_ref[...].astype(F32)
    total = total + c_ref[...].astype(F32) + d_ref[...].astype(F32)
    mixed = (x_ref[...].astype(F32) + total).astype(BF16)
    mixed_ref[...] = mixed
    m = mixed.astype(F32)
    scale = lax.rsqrt(jnp.mean(m * m, axis=1, keepdims=True) + norm_eps)
    normed_ref[...] = (m * scale * gain_ref[...]).astype(BF16)


def mix_and_norm(hidden_in, terms, norm_gain):
    rows, width = hidden_in.shape
    block = pl.BlockSpec((rows // 4, width), lambda i: (i, 0))
    return pl.pallas_call(
        mix_kernel,
        grid=(4,),
        in_specs=[block] * 5 + [pl.BlockSpec((1, width), lambda i: (0, 0))],
        out_specs=[block, block],
        out_shape=[jax.ShapeDtypeStruct((rows, width), BF16)] * 2,
        compiler_params=params(32),
        name="mix_norm",
    )(hidden_in, *terms, norm_gain.reshape(1, width))


def pick_kernel(base_s, routes_ref, weights_ref, rows_ref, x_ref, w_ref, *, local):
    rows = routes_ref.shape[2]
    slots = PACK * CAP
    upper = (
        lax.broadcasted_iota(jnp.int32, (rows, rows), 0)
        <= lax.broadcasted_iota(jnp.int32, (rows, rows), 1)
    ).astype(F32).astype(BF16)
    place = lax.broadcasted_iota(jnp.int32, (slots, 1), 0)
    columns, weight = [], 0.0
    for s in range(PACK):
        route = routes_ref[s]
        share = weights_ref[s]
        members, rates = [], []
        for e in range(local):
            hit = route == base_s[0] + e
            members.append(jnp.max(jnp.where(hit, 1.0, 0.0), axis=0, keepdims=True))
            rates.append(jnp.sum(jnp.where(hit, share, 0.0), axis=0, keepdims=True))
        member = jnp.concatenate(members, axis=0)
        counts = jnp.dot(member.astype(BF16), upper, preferred_element_type=F32)
        rank = jnp.where(member > 0.0, counts - 1.0, -1000.0).astype(jnp.int32)
        want = place - s * CAP
        hots = [want == rank[e : e + 1] for e in range(local)]
        weight = weight + jnp.concatenate(
            [
                jnp.sum(jnp.where(hots[e], rates[e], 0.0), axis=1, keepdims=True)
                for e in range(local)
            ],
            axis=0,
        )
        columns.append(
            jnp.concatenate([jnp.where(h, 1.0, 0.0) for h in hots], axis=0).astype(BF16)
        )
    hot = jnp.concatenate(columns, axis=1)
    picked = jnp.dot(hot, rows_ref[...], preferred_element_type=F32).astype(BF16)
    x_ref[...] = picked.reshape(x_ref.shape)
    w_ref[...] = weight.reshape(w_ref.shape)


def pick_rows(base, routes, weights, rows, local):
    senders, top, each = routes.shape
    width = rows.shape[1]
    slots = PACK * CAP
    steps = senders // PACK
    return pl.pallas_call(
        functools.partial(pick_kernel, local=local),
        grid_spec=pltpu.PrefetchScalarGridSpec(
            num_scalar_prefetch=1,
            grid=(steps,),
            in_specs=[
                pl.BlockSpec((PACK, top, each), lambda i, *_: (i, 0, 0)),
                pl.BlockSpec((PACK, top, each), lambda i, *_: (i, 0, 0)),
                pl.BlockSpec((PACK * each, width), lambda i, *_: (i, 0)),
            ],
            out_specs=[
                pl.BlockSpec((local, slots, width), lambda i, *_: (0, i, 0)),
                pl.BlockSpec((local, slots, 1), lambda i, *_: (0, i, 0)),
            ],
        ),
        out_shape=[
            jax.ShapeDtypeStruct((local, senders * CAP, width), BF16),
            jax.ShapeDtypeStruct((local, senders * CAP, 1), F32),
        ],
        compiler_params=params(48),
        cost_estimate=pl.CostEstimate(
            flops=2 * steps * local * slots * PACK * each * width,
            bytes_accessed=2 * (rows.size + local * senders * CAP * width),
            transcendentals=0,
        ),
        name="pick_rows",
    )(base, routes, weights, rows)


def expert_kernel(x_ref, w_ref, up_ref, down_ref, y_ref):
    x = x_ref[0]
    gate = jnp.dot(x, up_ref[0, 0], preferred_element_type=F32)
    up = jnp.dot(x, up_ref[0, 1], preferred_element_type=F32)
    act = ((up + 1.0) * gate * jax.nn.sigmoid(1.702 * gate)).astype(BF16)
    out = jnp.dot(act, down_ref[0], preferred_element_type=F32)
    y_ref[0] = (out * w_ref[0]).astype(BF16)


def run_experts(x, w, gate_up, down_proj, block):
    local, slots, width = x.shape
    units = down_proj.shape[1]
    return pl.pallas_call(
        expert_kernel,
        grid=(local, slots // block),
        in_specs=[
            pl.BlockSpec((1, block, width), lambda e, i: (e, i, 0)),
            pl.BlockSpec((1, block, 1), lambda e, i: (e, i, 0)),
            pl.BlockSpec((1, 2, width, units), lambda e, i: (e, 0, 0, 0)),
            pl.BlockSpec((1, units, width), lambda e, i: (e, 0, 0)),
        ],
        out_specs=pl.BlockSpec((1, block, width), lambda e, i: (e, i, 0)),
        out_shape=jax.ShapeDtypeStruct(x.shape, BF16),
        compiler_params=params(56),
        cost_estimate=pl.CostEstimate(
            flops=2 * 3 * local * slots * width * units,
            bytes_accessed=2 * (2 * x.size + gate_up.size + down_proj.size),
            transcendentals=local * slots * units,
        ),
        name="experts",
    )(x, w, gate_up, down_proj)


def spread_kernel(base_s, routes_ref, y_ref, out_ref, *, local):
    rows = routes_ref.shape[1]
    slots = PACK * CAP
    lower = (
        lax.broadcasted_iota(jnp.int32, (rows, rows), 1)
        <= lax.broadcasted_iota(jnp.int32, (rows, rows), 0)
    ).astype(F32).astype(BF16)
    place = lax.broadcasted_iota(jnp.int32, (1, slots), 1)
    y = y_ref[...].reshape(local * slots, y_ref.shape[2])
    hots = []
    for s in range(PACK):
        route = routes_ref[s]
        want = place - s * CAP
        pieces = []
        for e in range(local):
            hit = jnp.where(route == base_s[0] + e, 1.0, 0.0)
            member = jnp.max(hit, axis=1, keepdims=True)
            wide = jnp.broadcast_to(member, (rows, 128)).astype(BF16)
            counts = jnp.dot(lower, wide, preferred_element_type=F32)[:, :slots]
            rank = jnp.where(member > 0.0, counts - 1.0, -1000.0).astype(jnp.int32)
            pieces.append(jnp.where(rank == want, 1.0, 0.0))
        hots.append(jnp.concatenate(pieces, axis=1).astype(BF16))
    hot = jnp.concatenate(hots, axis=0)
    out_ref[...] = jnp.dot(hot, y, preferred_element_type=F32).astype(BF16)


def spread_rows(base, routes, y):
    senders, each, top = routes.shape
    local, _, width = y.shape
    slots = PACK * CAP
    steps = senders // PACK
    return pl.pallas_call(
        functools.partial(spread_kernel, local=local),
        grid_spec=pltpu.PrefetchScalarGridSpec(
            num_scalar_prefetch=1,
            grid=(steps,),
            in_specs=[
                pl.BlockSpec((PACK, each, top), lambda i, *_: (i, 0, 0)),
                pl.BlockSpec((local, slots, width), lambda i, *_: (0, i, 0)),
            ],
            out_specs=pl.BlockSpec((PACK * each, width), lambda i, *_: (i, 0)),
        ),
        out_shape=jax.ShapeDtypeStruct((senders * each, width), BF16),
        compiler_params=params(48),
        cost_estimate=pl.CostEstimate(
            flops=2 * steps * local * slots * PACK * each * width,
            bytes_accessed=2 * (y.size + senders * each * width),
            transcendentals=0,
        ),
        name="spread_rows",
    )(base, routes, y)


def exchange(value, axes, count, step):
    return lax.ppermute(value, axes, [(i, i ^ step) for i in range(count)])


def attention_and_norm(
    hidden_in, queries, kv_pages, page_table, new_rows, context, sink_logits, out_proj, norm_gain,
    dp, dp_count,
):
    me = lax.axis_index(dp)
    order = list(range(dp_count - 1, 0, -1)) + [0]
    arrived = {}
    for step in order:
        col = (me ^ step).astype(jnp.int32).reshape(1)
        part = attend_group(
            col, queries, kv_pages, page_table, new_rows, context, sink_logits, dp_count
        )
        arrived[step] = exchange(part, dp, dp_count, step) if step else part
    terms = []
    for step in order:
        term = jnp.dot(arrived[step], out_proj, preferred_element_type=F32).astype(BF16)
        terms.append(exchange(term, dp, dp_count, step) if step else term)
    return mix_and_norm(hidden_in, terms, norm_gain)


def layer_gathered(
    hidden_in, queries, kv_pages, page_table, new_rows, context, sink_logits, out_proj, norm_gain,
    routes, route_weights, gate_up, down_proj, *, sizes,
):
    ny, nx, nz, nc = sizes
    everyone = ("y", "x", "z", "core")
    each, top = routes.shape
    local = gate_up.shape[0]
    base = ((lax.axis_index("z") * nc + lax.axis_index("core")) * local).astype(jnp.int32)
    base = base.reshape(1)

    def by_core(info):
        info = lax.all_gather(info, everyone, axis=0, tiled=False)
        info = info.reshape((ny * nx * nz, nc) + info.shape[1:])
        return jnp.swapaxes(info, 0, 1).reshape((ny * nx * nz * nc,) + info.shape[2:])

    all_routes = by_core(routes)
    all_routes_t = jnp.swapaxes(all_routes, 1, 2)
    all_weights_t = jnp.swapaxes(by_core(route_weights), 1, 2)
    mixed, normed = attention_and_norm(
        hidden_in, queries, kv_pages, page_table, new_rows, context, sink_logits, out_proj,
        norm_gain, ("y", "x"), ny * nx,
    )
    rows = lax.all_gather(normed, "z", axis=0, tiled=True)
    rows = lax.all_gather(rows, ("y", "x"), axis=0, tiled=True)
    rows = lax.all_gather(rows, "core", axis=0, tiled=True)
    x, w = pick_rows(base, all_routes_t, all_weights_t, rows, local)
    y = run_experts(x, w, gate_up, down_proj, x.shape[1] // 2)
    total = spread_rows(base, all_routes, y)
    total = lax.psum_scatter(total, "core", scatter_dimension=0, tiled=True)
    total = lax.psum_scatter(total, ("y", "x"), scatter_dimension=0, tiled=True)
    total = lax.psum_scatter(total, "z", scatter_dimension=0, tiled=True)
    return (mixed.astype(F32) + total.astype(F32)).astype(BF16)


def layer_sent(
    hidden_in, queries, kv_pages, page_table, new_rows, context, sink_logits, out_proj, norm_gain,
    routes, route_weights, gate_up, down_proj, *, dp_count,
):
    row_count, model_width = hidden_in.shape
    mixed, normed = attention_and_norm(
        hidden_in, queries, kv_pages, page_table, new_rows, context, sink_logits, out_proj,
        norm_gain, "dp", dp_count,
    )
    assign = routes.reshape(-1)
    onehot = (assign[:, None] == jnp.arange(E, dtype=jnp.int32)[None, :]).astype(jnp.int32)
    slot_index = jnp.sum((jnp.cumsum(onehot, axis=0) - onehot) * onehot, axis=1)
    source = jnp.arange(assign.shape[0], dtype=jnp.int32) // routes.shape[1]
    send_rows = jnp.zeros((E, CAP, model_width), BF16).at[assign, slot_index].set(normed[source])
    copies = jnp.broadcast_to(send_rows[None], (dp_count,) + send_rows.shape)
    copies = copies.reshape(dp_count * E, CAP, model_width)
    everyone = ("dp", "expert")
    blocks = lax.all_to_all(copies, everyone, split_axis=0, concat_axis=0, tiled=True)
    local = gate_up.shape[0]
    shape = blocks.shape
    blocks = blocks.reshape(shape[0] // local, local, CAP, model_width)
    gate_up_f = jnp.einsum("sjcd,jtdf->sjctf", blocks, gate_up, preferred_element_type=F32)
    gate, up = gate_up_f[:, :, :, 0, :], gate_up_f[:, :, :, 1, :]
    hidden = ((up + 1.0) * gate * jax.nn.sigmoid(1.702 * gate)).astype(BF16)
    partials = jnp.einsum("sjcf,jfd->sjcd", hidden, down_proj, preferred_element_type=F32)
    partials = partials.astype(BF16).reshape(shape)
    back = lax.all_to_all(partials, everyone, split_axis=0, concat_axis=0, tiled=True)
    back = jnp.sum(back.reshape(dp_count, E, CAP, model_width).astype(F32), axis=0)
    picked = back[assign, slot_index] * route_weights.reshape(-1)[:, None]
    mix = jnp.sum(picked.reshape(row_count, routes.shape[1], model_width), axis=1)
    return (mixed.astype(F32) + mix).astype(BF16)


def solution(mesh):
    dp_count, expert_count = mesh.shape["dp"], mesh.shape["expert"]
    if dp_count == 4 and expert_count == 8:
        sizes = (2, 2, 4, 2)
        grid = Mesh(mesh.devices.reshape(sizes), ("y", "x", "z", "core"))
        dp, expert, body = ("y", "x"), ("z", "core"), functools.partial(layer_gathered, sizes=sizes)
    else:
        grid = mesh
        dp, expert, body = ("dp",), ("expert",), functools.partial(layer_sent, dp_count=dp_count)
    everyone = dp + expert
    return jax.shard_map(
        body,
        mesh=grid,
        in_specs=(
            P(everyone, None),
            P(everyone, None),
            P(everyone, None, None),
            P(everyone, None),
            P(everyone),
            P(everyone),
            P(),
            P(dp, None),
            P(),
            P(everyone, None),
            P(everyone, None),
            P(expert, None, None, dp),
            P(expert, dp, None),
        ),
        out_specs=P(everyone, None),
        check_vma=False,
    )
```

time: 1290 us -> 677 us (0.52)
  blocking collectives: 417 us -> 77.6 us
  local copies, waits for them, and re-layouts: 190 us -> 40.1 us
  matrix products: 144 us -> 8.54 us
  Pallas kernels: 0 us -> 117 us
  other arithmetic: 70.6 us -> 1.3 us
  waiting for transfers between devices: 432 us -> 410 us
  loops' own time: 17.4 us -> 0 us
    all_to_all x2 -> x0, blocking collectives: 417 us -> none  [the longest x1 397 us: per_device(): lax.all_to_all(copies, ('dp', 'expert'), split_axis=0, concat_axis=0, til...]
    all_to_all x1 -> x0, waiting for transfers between devices: 392 us -> none  [per_device(): lax.all_to_all(partials, ('dp', 'expert'), split_axis=0, concat_axis=0, t...]
    reduce_scatter x0 -> x2, waiting for transfers between devices: none -> 181 us  [the longest x1 121 us: layer_gathered(): total = lax.psum_scatter(total, ('y', 'x'), scatter_dimension=0, tiled=True)]
    all_gather x0 -> x3, waiting for transfers between devices: none -> 180 us  [the longest x1 119 us: layer_gathered(): rows = lax.all_gather(rows, ('y', 'x'), axis=0, tiled=True)]
    dot_general x19 -> x4, matrix products: 144 us -> 8.54 us  [attention_and_norm(): jnp.dot(arrived[step], out_proj, preferred_element_type=F32).astype(BF16)]
    pallas_call x0 -> x8, Pallas kernels: none -> 117 us  [the longest x1 38.7 us: run_experts(): pl.pallas_call(expert_kernel, grid=(local, slots // block), in_specs=[pl....]
    scatter x2 -> x0, local copies, waits for them, and re-layouts: 115 us -> none  [per_device(): jnp.zeros((E, CAP, model_width), jnp.bfloat16).at[assign, slot_index]]
    all_gather x0 -> x2, blocking collectives: none -> 77.6 us  [by_core(): info = lax.all_gather(info, everyone, axis=0, tiled=False)]
  transfers between devices with their start and end apart: 2 -> 12, of which waited for: 2 -> 8; matrix products, arithmetic and copies ran while one was open for 0% -> 4% of each run, Pallas kernels for 0% -> 4%
where the time goes in v1:
time: 677 us; the launch traced here: 676 us
  waiting for transfers between devices  410 us (61%)
  Pallas kernels  117 us (17%)
  blocking collectives  77.6 us (11%)
  local copies, waits for them, and re-layouts  40.1 us (6%)
  between operations  13.7 us (2%)
  matrix products  8.54 us (1%)
  starting transfers between devices  8.44 us (1%)
    reduce_scatter x1, waiting for transfers between devices, layer_gathered(): total = lax.psum_scatter(total, ('y', 'x'), scatter_dimension=0, tiled=True)  121 us
    all_gather x1, waiting for transfers between devices, layer_gathered(): rows = lax.all_gather(rows, ('y', 'x'), axis=0, tiled=True)  119 us
    all_gather x2, blocking collectives, by_core(): info = lax.all_gather(info, everyone, axis=0, tiled=False)  77.6 us
    all_gather x1, waiting for transfers between devices, layer_gathered(): rows = lax.all_gather(normed, 'z', axis=0, tiled=True)  61.5 us
    reduce_scatter x1, waiting for transfers between devices, layer_gathered(): total = lax.psum_scatter(total, 'z', scatter_dimension=0, tiled=True)  60.4 us
    pallas_call x1, Pallas kernels, run_experts(): pl.pallas_call(expert_kernel, grid=(local, slots // block), in_specs=[pl....  38.7 us
    pallas_call x4, Pallas kernels, attend_group(): pl.pallas_call(body, grid_spec=pltpu.PrefetchScalarGridSpec(num_scalar_pr...  35.5 us
    unnamed x7, waiting for transfers between devices  32.7 us
  transfers between devices with their start and end apart: 12, of which 8 were waited for; matrix products, arithmetic and copies ran while one was open for 4% of the time, Pallas kernels for 4%

profile of v1, /device:TPU:0, one launch (start us, length us, event | category | flops | bytes accessed | tf_op | source)
XLA Modules:
  0.0 676.1 jit_solution(11466931188392447265)
XLA Ops:
  6.5 0.8 reshape.37.table_s
  7.3 2.2 copy-done.4
  9.5 1.2 copy-done.7
  10.8 0.7 copy-done.9
  11.4 0.7 copy-done.11
  12.1 0.7 copy-done.13
  12.7 8.8 %attend.4 = bf16[128,1024]{1,0:T(8,128)(2,1)S(1)} custom-call(s32[1]{0:T(128)} %bitcast.col_s, s32[4]{0:T(128)S(1)} %copy-done.9, s32[4]{0:T(128)S(1)} %copy-done.11, s32[16]{0:T(128)S(1)} %reshape.37.table_s, f32[64]{0:T(128)S(1)} %copy-done.13, bf16[128,4096]{1,0:T(8,128)(2,1)S(1)} %copy-done.7, bf16[16,128,1024]{2,1,0:T(8,128)(2,1)S(1)} %copy-done.4), custom_call_target="tpu_custom_call" | custom-call | flops 2147483648 | bytes 1572864 | tf_op jit(solution)/shard_map/attend/pallas_call | solution.py:104
  21.6 4.0 collective-permute-start
  25.5 2.2 copy-done.5
  27.7 8.8 %attend.5 = bf16[128,1024]{1,0:T(8,128)(2,1)S(1)} custom-call(s32[1]{0:T(128)} %bitcast.1.col_s, s32[4]{0:T(128)S(1)} %copy-done.10, s32[4]{0:T(128)S(1)} %copy-done.12, s32[16]{0:T(128)S(1)} %reshape.37.table_s, f32[64]{0:T(128)S(1)} %copy-done.14, bf16[128,4096]{1,0:T(8,128)(2,1)S(1)} %copy-done.8, bf16[16,128,1024]{2,1,0:T(8,128)(2,1)S(1)} %copy-done.5), custom_call_target="tpu_custom_call" | custom-call | flops 2147483648 | bytes 1572864 | tf_op jit(solution)/shard_map/attend/pallas_call | solution.py:104
  36.5 0.6 collective-permute-start.2
  37.1 2.2 copy-done.6
  39.3 8.8 %attend.6 = bf16[128,1024]{1,0:T(8,128)(2,1)S(1)} custom-call(s32[1]{0:T(128)} %bitcast.2.col_s, s32[4]{0:T(128)S(1)} %copy-done.10, s32[4]{0:T(128)S(1)} %copy-done.12, s32[16]{0:T(128)S(1)} %reshape.37.table_s, f32[64]{0:T(128)S(1)} %copy-done.14, bf16[128,4096]{1,0:T(8,128)(2,1)S(1)} %copy-done.8, bf16[16,128,1024]{2,1,0:T(8,128)(2,1)S(1)} %copy-done.6), custom_call_target="tpu_custom_call" | custom-call | flops 2147483648 | bytes 1572864 | tf_op jit(solution)/shard_map/attend/pallas_call | solution.py:104
  48.3 1.7 convolution_convert_fusion.3
  50.0 2.9 collective-permute-start.1
  53.0 2.6 convolution_convert_fusion.2
  55.5 0.5 collective-permute-start.3
  56.0 1.4 collective-permute-done.4
  57.4 2.6 convolution_convert_fusion.1
  60.1 9.0 %attend.7 = bf16[128,1024]{1,0:T(8,128)(2,1)S(1)} custom-call(s32[1]{0:T(128)} %bitcast.3.col_s, s32[4]{0:T(128)S(1)} %copy-done.10, s32[4]{0:T(128)S(1)} %copy-done.12, s32[16]{0:T(128)S(1)} %reshape.37.table_s, f32[64]{0:T(128)S(1)} %copy-done.14, bf16[128,4096]{1,0:T(8,128)(2,1)S(1)} %copy-done.8, bf16[16,128,1024]{2,1,0:T(8,128)(2,1)S(1)} %copy-done.6), custom_call_target="tpu_custom_call" | custom-call | flops 2147483648 | bytes 1572864 | tf_op jit(solution)/shard_map/attend/pallas_call | solution.py:104
  69.1 1.7 convolution_convert_fusion
  71.2 0.4 copy.34.x_ref
  71.6 2.8 collective-permute-done.1
  74.4 1.5 copy.35.a_ref
  75.8 11.8 %collective-permute-done.3 = bf16[128,2880]{0,1:T(8,128)(2,1)} collective-permute-done((bf16[128,2880]{0,1:T(8,128)(2,1)}, bf16[128,2880]{0,1:T(8,128)(2,1)}, u32[]{:S(2)}, u32[]{:S(2)}) %collective-permute-start.3) | collective-permute-done | bytes 737312 | tf_op jit(solution)/shard_map/ppermute | solution.py:311
  87.7 1.5 copy.36.b_ref
  89.2 2.3 copy.37.c_ref
  91.5 1.1 copy-done
  92.6 1.1 mix_norm.1
  93.7 0.9 copy-done.1
  94.6 0.9 copy-done.3
  95.5 61.5 %all-gather.6.cloned.1.call-done = bf16[512,2880]{1,0:T(8,128)(2,1)} async-done(((bf16[128,2880]{1,0:T(8,128)(2,1)}), bf16[512,2880]{1,0:T(8,128)(2,1)}) %all-gather.6.cloned.1.call-update) | async-done | bytes 2949136 | tf_op jit(solution)/shard_map/all_gather | solution.py:357
  157.1 118.6 %all-gather.8.cloned.1.call-done = bf16[2048,2880]{1,0:T(8,128)(2,1)} async-done(((bf16[512,2880]{1,0:T(8,128)(2,1)}), bf16[2048,2880]{1,0:T(8,128)(2,1)}) %all-gather.8.cloned.1.call-update) | async-done | bytes 11796496 | tf_op jit(solution)/shard_map/all_gather | solution.py:358
  275.8 0.6 copy-done.19
  276.4 40.7 %all-gather = s32[4096,4]{0,1:T(4,128)S(1)} all-gather(s32[128,4]{0,1:T(4,128)S(1)} %copy-done.19), channel_id=2, replica_groups=mesh['y'=2,'x'=2,'z'=4,'core'=2] {'y','x','z','core'}, dimensions={0}, use_global_device_ids=true | all-gather | bytes 67584 | tf_op jit(solution)/shard_map/all_gather | solution.py:346
  317.2 36.9 %all-gather.1 = f32[4096,4]{0,1:T(4,128)S(1)} all-gather(f32[128,4]{0,1:T(4,128)S(1)} %copy-done.20), channel_id=3, replica_groups=mesh['y'=2,'x'=2,'z'=4,'core'=2] {'y','x','z','core'}, dimensions={0}, use_global_device_ids=true | all-gather | bytes 67584 | tf_op jit(solution)/shard_map/all_gather | solution.py:346
  354.2 0.6 copy.39
  354.8 0.6 copy.41.routes_ref
  355.5 16.4 %copy.42.down_ref = bf16[4,512,2880]{2,1,0:T(8,128)(2,1)} copy(bf16[4,512,2880]{1,2,0:T(8,128)(2,1)} %param.25) | data formatting | bytes 23592960 | tf_op args[12]
  371.9 19.1 %pick_rows.1 = (bf16[4,640,2880]{2,1,0:T(8,128)(2,1)}, f32[4,640,1]{2,1,0:T(8,128)S(1)}) custom-call(s32[1]{0:T(128)} %bitcast.4.base_s, s32[32,4,128]{2,1,0:T(4,128)S(1)} %copy.41.routes_ref, f32[32,4,128]{2,1,0:T(4,128)S(1)} %bitcast.30, bf16[4096,2880]{1,0:T(8,128)(2,1)} %all-gather.10.cloned.1.call-done.rows_ref), custom_call_target="tpu_custom_call" | custom-call | flops 7549747200 | bytes 38338560 | tf_op jit(solution)/shard_map/pick_rows/pallas_call | solution.py:195
  390.9 1.1 copy-done.15
  392.0 38.7 %experts.1.y_ref = bf16[4,640,2880]{2,1,0:T(8,128)(2,1)} custom-call(bf16[4,640,2880]{2,1,0:T(8,128)(2,1)} %get-tuple-element.11.x_ref, f32[4,640,1]{2,1,0:T(8,128)} %copy-done.15, bf16[4,2,2880,512]{3,2,1,0:T(8,128)(2,1)} %up_ref.1, bf16[4,512,2880]{2,1,0:T(8,128)(2,1)} %copy.42.down_ref), custom_call_target="tpu_custom_call" | custom-call | flops 22649241600 | bytes 64880640 | tf_op jit(solution)/shard_map/experts/pallas_call | solution.py:236
  430.7 22.3 %spread_rows.1 = bf16[4096,2880]{1,0:T(8,128)(2,1)} custom-call(s32[1]{0:T(128)} %bitcast.4.base_s, s32[32,128,4]{2,1,0:T(8,128)S(1)} %bitcast.29, bf16[4,640,2880]{2,1,0:T(8,128)(2,1)} %experts.1.y_ref), custom_call_target="tpu_custom_call" | custom-call | flops 7549747200 | bytes 38338560 | tf_op jit(solution)/shard_map/spread_rows/pallas_call | solution.py:288
  453.0 32.7 %reduce-scatter.11.cloned.1.call-done = bf16[2048,2880]{1,0:T(8,128)(2,1)} async-done(((bf16[4096,2880]{1,0:T(8,128)(2,1)}), bf16[2048,2880]{1,0:T(8,128)(2,1)}) %reduce-scatter.11.cloned.1.call-update) | async-done | bytes 11796496
  485.8 120.6 %reduce-scatter.7.cloned.1.call-done = bf16[512,2880]{1,0:T(8,128)(2,1)} async-done(((bf16[2048,2880]{1,0:T(8,128)(2,1)}), bf16[512,2880]{1,0:T(8,128)(2,1)}) %reduce-scatter.7.cloned.1.call-update) | async-done | bytes 2949136 | tf_op jit(solution)/shard_map/reduce_scatter | solution.py:364
  606.4 60.4 %reduce-scatter.9.cloned.1.call-done = bf16[128,2880]{1,0:T(8,128)(2,1)} async-done(((bf16[512,2880]{1,0:T(8,128)(2,1)}), bf16[128,2880]{1,0:T(8,128)(2,1)}) %reduce-scatter.9.cloned.1.call-update) | async-done | bytes 737296 | tf_op jit(solution)/shard_map/reduce_scatter | solution.py:365
  666.8 1.3 add_convert_fusion
  668.1 1.1 copy.43
  (53 shorter events, 1.2 us)
Async XLA Ops:
  6.5 19.0 %copy-start.14 = (f32[64]{0:T(128)S(1)}, f32[64]{0:T(128)}, u32[]{:S(2)}) copy-start(f32[64]{0:T(128)} %sink_s.7) | copy-start | bytes 772
  6.5 19.0 %copy-start.12 = (s32[4]{0:T(128)S(1)}, s32[4]{0:T(128)}, u32[]{:S(2)}) copy-start(s32[4]{0:T(128)} %ctx_s.7) | copy-start | bytes 52
  6.5 19.0 %copy-start.10 = (s32[4]{0:T(128)S(1)}, s32[4]{0:T(128)}, u32[]{:S(2)}) copy-start(s32[4]{0:T(128)} %rows_s.7) | copy-start | bytes 52
  6.5 150.4 %all-gather.6.cloned.1.call-start = ((), (), s32[]{:S(2)}) async-start(), calls=%async_computation.3 | async-start | bytes 3768320 | tf_op jit(solution)/shard_map/all_gather | solution.py:357
  7.3 2.2 copy-start.4
  9.5 1.2 copy-start.7
  10.8 0.7 copy-start.9
  11.4 0.7 copy-start.11
  12.1 0.7 copy-start.13
  12.7 12.8 %copy-start.8 = (bf16[128,4096]{1,0:T(8,128)(2,1)S(1)}, bf16[128,4096]{1,0:T(8,128)(2,1)}, u32[]{:S(2)}) copy-start(bf16[128,4096]{1,0:T(8,128)(2,1)} %q_ref.7) | copy-start | bytes 3145732
  21.6 26.7 %collective-permute-start = (bf16[128,1024]{1,0:T(8,128)(2,1)S(1)}, bf16[128,1024]{1,0:T(8,128)(2,1)S(1)}, u32[]{:S(2)}, u32[]{:S(2)}) collective-permute-start(bf16[128,1024]{1,0:T(8,128)(2,1)S(1)} %attend.4), channel_id=1, source_target_pairs={{0,24},{8,16},{16,8},{24,0},{1,25},{9,17},{17,9},{25,1},{2,26},{10... | collective-permute-start | bytes 786440 | tf_op jit(solution)/shard_map/ppermute | solution.py:311
  25.5 2.2 copy-start.5
  36.5 16.4 %collective-permute-start.2 = (bf16[128,1024]{1,0:T(8,128)(2,1)S(1)}, bf16[128,1024]{1,0:T(8,128)(2,1)S(1)}, u32[]{:S(2)}, u32[]{:S(2)}) collective-permute-start(bf16[128,1024]{1,0:T(8,128)(2,1)S(1)} %attend.5), channel_id=1, source_target_pairs={{0,16},{8,24},{16,0},{24,8},{1,17},{9,25},{17,1},{25,9},{2,18},{10... | collective-permute-start | bytes 786440 | tf_op jit(solution)/shard_map/ppermute | solution.py:311
  37.1 2.2 copy-start.6
  39.3 9.0 %copy-start.16 = (bf16[1024,2880]{0,1:T(8,128)(2,1)S(1)}, bf16[1024,2880]{0,1:T(8,128)(2,1)}, u32[]{:S(2)}) copy-start(bf16[1024,2880]{0,1:T(8,128)(2,1)} %param.20) | copy-start | bytes 17694724
  48.1 9.3 %collective-permute-start.4 = (bf16[128,1024]{1,0:T(8,128)(2,1)S(1)}, bf16[128,1024]{1,0:T(8,128)(2,1)S(1)}, u32[]{:S(2)}, u32[]{:S(2)}) collective-permute-start(bf16[128,1024]{1,0:T(8,128)(2,1)S(1)} %attend.6), channel_id=1, source_target_pairs={{0,8},{8,0},{16,24},{24,16},{1,9},{9,1},{17,25},{25,17},{2,10},{10... | collective-permute-start | bytes 786440 | tf_op jit(solution)/shard_map/ppermute | solution.py:311
  50.0 24.3 %collective-permute-start.1 = (bf16[128,2880]{0,1:T(8,128)(2,1)S(1)}, bf16[128,2880]{0,1:T(8,128)(2,1)}, u32[]{:S(2)}, u32[]{:S(2)}) collective-permute-start(bf16[128,2880]{0,1:T(8,128)(2,1)S(1)} %convolution_convert_fusion.3), channel_id=1, source_target_pairs={{0,24},{8,16},{16,8},{24,0},{1,25},{9,17},{17,9},{25,1},{2,26},{10... | collective-permute-start | bytes 2211848 | tf_op jit(solution)/shard_map/ppermute | solution.py:311
  55.5 4.6 copy-start.18
  55.5 32.1 %collective-permute-start.3 = (bf16[128,2880]{0,1:T(8,128)(2,1)}, bf16[128,2880]{0,1:T(8,128)(2,1)}, u32[]{:S(2)}, u32[]{:S(2)}) collective-permute-start(bf16[128,2880]{0,1:T(8,128)(2,1)} %convolution_convert_fusion.2), channel_id=1, source_target_pairs={{0,16},{8,24},{16,0},{24,8},{1,17},{9,25},{17,1},{25,9},{2,18},{10... | collective-permute-start | bytes 2211848 | tf_op jit(solution)/shard_map/ppermute | solution.py:311
  60.0 29.1 %collective-permute-start.5 = (bf16[128,2880]{0,1:T(8,128)(2,1)}, bf16[128,2880]{0,1:T(8,128)(2,1)}, u32[]{:S(2)}, u32[]{:S(2)}) collective-permute-start(bf16[128,2880]{0,1:T(8,128)(2,1)} %convolution_convert_fusion.1), channel_id=1, source_target_pairs={{0,8},{8,0},{16,24},{24,16},{1,9},{9,1},{17,25},{25,17},{2,10},{10... | collective-permute-start | bytes 2211848 | tf_op jit(solution)/shard_map/ppermute | solution.py:311
  69.1 2.1 copy-start.17
  91.5 1.1 copy-start
  93.7 0.9 copy-start.1
  94.6 0.9 copy-start.3
  95.5 180.2 %all-gather.8.cloned.1.call-start = ((), (), s32[]{:S(2)}) async-start(), calls=%async_computation.4 | async-start | bytes 15073280 | tf_op jit(solution)/shard_map/all_gather | solution.py:358
  157.0 214.9 %all-gather.10.cloned.1.call-start = ((), (), s32[]{:S(2)}) async-start(), calls=%async_computation.5 | async-start | bytes 36175872 | tf_op jit(solution)/shard_map/all_gather | solution.py:359
  275.7 0.7 copy-start.19
  275.7 41.5 %copy-start.20 = (f32[128,4]{0,1:T(4,128)S(1)}, f32[128,4]{0,1:T(4,128)}, u32[]{:S(2)}) copy-start(f32[128,4]{0,1:T(4,128)} %param.23) | copy-start | bytes 6148
  275.7 210.0 %reduce-scatter.11.cloned.1.call-start = ((), (), s32[]{:S(2)}) async-start(), calls=%async_computation.8 | async-start | bytes 36175872
  390.9 1.1 copy-start.15
  453.0 153.4 %reduce-scatter.7.cloned.1.call-start = ((), (), s32[]{:S(2)}) async-start(), calls=%async_computation.6 | async-start | bytes 15073280 | tf_op jit(solution)/shard_map/reduce_scatter | solution.py:364
  485.7 181.1 %copy-start.2 = (bf16[128,2880]{1,0:T(8,128)(2,1)S(1)}, bf16[128,2880]{1,0:T(8,128)(2,1)}, u32[]{:S(2)}) copy-start(bf16[128,2880]{1,0:T(8,128)(2,1)} %copy-done.1) | copy-start | bytes 2211844
  485.7 181.1 %reduce-scatter.9.cloned.1.call-start = ((), (), s32[]{:S(2)}) async-start(), calls=%async_computation.7 | async-start | bytes 3768320 | tf_op jit(solution)/shard_map/reduce_scatter | solution.py:365
Sparse Core Ops, SparseCore 0:
  95.6 61.3 all-gather.5
  158.8 116.8 all-gather.7
  277.2 38.9 all-gather.9
  453.1 32.5 reduce-scatter.10
  488.7 117.6 reduce-scatter.6
  608.5 58.1 reduce-scatter.8

commit v2 on v1

--- a/solution.py
+++ b/solution.py
@@ -15,7 +15,7 @@
 CAP = 20
 GROUP = QH // KVH
 TILE = 32
-PACK = 4
+VMEM_MIB = 58
 
 norm_eps = 1e-05
 F32 = jnp.float32
@@ -115,7 +115,7 @@
             out_specs=pl.BlockSpec((rows, q_width), lambda i, *_: (0, 0)),
         ),
         out_shape=jax.ShapeDtypeStruct((rows, q_width), BF16),
-        compiler_params=params(32),
+        compiler_params=params(VMEM_MIB),
         cost_estimate=pl.CostEstimate(
             flops=8 * flops,
             bytes_accessed=2 * (2 * rows * q_width + pages * page_len * kv_width // groups),
@@ -131,39 +131,63 @@
     mixed = (x_ref[...].astype(F32) + total).astype(BF16)
     mixed_ref[...] = mixed
     m = mixed.astype(F32)
-    scale = lax.rsqrt(jnp.mean(m * m, axis=1, keepdims=True) + norm_eps)
-    normed_ref[...] = (m * scale * gain_ref[...]).astype(BF16)
-
-
-def mix_and_norm(hidden_in, terms, norm_gain):
-    rows, width = hidden_in.shape
-    block = pl.BlockSpec((rows // 4, width), lambda i: (i, 0))
+    scale = lax.rsqrt(jnp.mean(m * m, axis=0, keepdims=True) + norm_eps)
+    normed = (jnp.transpose(m * scale) * gain_ref[...]).astype(BF16)
+    rows, width = normed.shape
+    normed_ref[:, :width] = normed
+    if normed_ref.shape[1] > width:
+        normed_ref[:, width:] = jnp.zeros((rows, normed_ref.shape[1] - width), BF16)
+
+
+def mix_and_norm(hidden_t, terms_t, norm_gain):
+    width, rows = hidden_t.shape
+    normed = jax.ShapeDtypeStruct((rows, -(-width // 128) * 128), BF16)
     return pl.pallas_call(
         mix_kernel,
-        grid=(4,),
-        in_specs=[block] * 5 + [pl.BlockSpec((1, width), lambda i: (0, 0))],
-        out_specs=[block, block],
-        out_shape=[jax.ShapeDtypeStruct((rows, width), BF16)] * 2,
-        compiler_params=params(32),
+        out_shape=[jax.ShapeDtypeStruct((width, rows), BF16), normed],
+        compiler_params=params(VMEM_MIB),
         name="mix_norm",
-    )(hidden_in, *terms, norm_gain.reshape(1, width))
-
-
-def pick_kernel(base_s, routes_ref, weights_ref, rows_ref, x_ref, w_ref, *, local):
-    rows = routes_ref.shape[2]
-    slots = PACK * CAP
+    )(hidden_t, *terms_t, norm_gain.reshape(1, width))
+
+
+def finish_kernel(mixed_ref, *refs):
+    parts, out_ref = refs[:-1], refs[-1]
+    total = parts[0][...].astype(F32)
+    for part in parts[1:]:
+        total = total + part[...].astype(F32)
+    total = jnp.transpose(total)[: mixed_ref.shape[0]]
+    out_ref[...] = (mixed_ref[...].astype(F32) + total).astype(BF16)
+
+
+def finish(mixed_t, parts):
+    return pl.pallas_call(
+        finish_kernel,
+        out_shape=jax.ShapeDtypeStruct(mixed_t.shape, BF16),
+        compiler_params=params(VMEM_MIB),
+        name="finish",
+    )(mixed_t, *parts)
+
+
+def back_order():
+    return [3, 1, 2, 0]
+
+
+def pick_plane(base, info_ref, plane, rows, x_ref, w_ref, hot_ref, *, local, count):
+    each = info_ref.shape[2]
+    top = info_ref.shape[1] // 2
+    slots = count * CAP
     upper = (
-        lax.broadcasted_iota(jnp.int32, (rows, rows), 0)
-        <= lax.broadcasted_iota(jnp.int32, (rows, rows), 1)
+        lax.broadcasted_iota(jnp.int32, (each, each), 0)
+        <= lax.broadcasted_iota(jnp.int32, (each, each), 1)
     ).astype(F32).astype(BF16)
     place = lax.broadcasted_iota(jnp.int32, (slots, 1), 0)
     columns, weight = [], 0.0
-    for s in range(PACK):
-        route = routes_ref[s]
-        share = weights_ref[s]
+    for s in range(count):
+        info = info_ref[plane * count + s]
+        route, share = info[:top], info[top:]
         members, rates = [], []
         for e in range(local):
-            hit = route == base_s[0] + e
+            hit = route == (base + e).astype(F32)
             members.append(jnp.max(jnp.where(hit, 1.0, 0.0), axis=0, keepdims=True))
             rates.append(jnp.sum(jnp.where(hit, share, 0.0), axis=0, keepdims=True))
         member = jnp.concatenate(members, axis=0)
@@ -178,137 +202,137 @@
             ],
             axis=0,
         )
-        columns.append(
-            jnp.concatenate([jnp.where(h, 1.0, 0.0) for h in hots], axis=0).astype(BF16)
+        columns.append(jnp.concatenate([jnp.where(h, 1.0, 0.0) for h in hots], axis=0))
+    for i, s in enumerate(back_order()):
+        hot_ref[plane, i * each : (i + 1) * each, :] = jnp.transpose(columns[s]).astype(BF16)
+    hot = jnp.concatenate([c.astype(BF16) for c in columns], axis=1)
+    picked = jnp.dot(hot, rows, preferred_element_type=F32).astype(BF16)[:, : x_ref.shape[2]]
+    for e in range(local):
+        x_ref[e, plane * slots : (plane + 1) * slots, :] = picked[e * slots : (e + 1) * slots]
+        w_ref[e, plane * slots : (plane + 1) * slots, :] = jnp.broadcast_to(
+            weight[e * slots : (e + 1) * slots], (slots, 128)
         )
-    hot = jnp.concatenate(columns, axis=1)
-    picked = jnp.dot(hot, rows_ref[...], preferred_element_type=F32).astype(BF16)
-    x_ref[...] = picked.reshape(x_ref.shape)
-    w_ref[...] = weight.reshape(w_ref.shape)
-
-
-def pick_rows(base, routes, weights, rows, local):
-    senders, top, each = routes.shape
-    width = rows.shape[1]
-    slots = PACK * CAP
-    steps = senders // PACK
+
+
+def chunk_kernel(
+    base_s, info_ref, *refs, local, count, splits, held, passed,
+):
+    pieces, refs = refs[:held], refs[held:]
+    up_ref, down_ref, refs = refs[0], refs[1], refs[2 + passed :]
+    mine_out, far_out, other_out, refs = refs[0], refs[1], refs[2], refs[3 + passed :]
+    x_ref, w_ref, hot_ref, acc_ref, y_ref = refs
+    step = pl.program_id(0)
+    e = step // splits
+    part_at = step % splits
+    slots = count * CAP
+
+    @pl.when(step == 0)
+    def _():
+        for plane in (0, 1):
+            rows = [ref[...] for ref in pieces[plane * held // 2 : (plane + 1) * held // 2]]
+            rows = jnp.concatenate(rows, axis=0)
+            pick_plane(
+                base_s[0], info_ref, plane, rows, x_ref, w_ref, hot_ref,
+                local=local, count=count,
+            )
+
+    x = x_ref[e]
+    gate = jnp.dot(x, up_ref[0, 0], preferred_element_type=F32)
+    up = jnp.dot(x, up_ref[0, 1], preferred_element_type=F32)
+    act = ((up + 1.0) * gate * jax.nn.sigmoid(1.702 * gate)).astype(BF16)
+    part = lax.dot_general(
+        act, down_ref[0], (((1,), (1,)), ((), ())), preferred_element_type=F32
+    )
+
+    @pl.when(part_at == 0)
+    def _():
+        acc_ref[...] = part
+
+    @pl.when(part_at > 0)
+    def _():
+        acc_ref[...] += part
+
+    @pl.when(part_at == splits - 1)
+    def _():
+        y = (acc_ref[...] * w_ref[e][:, :1]).astype(BF16)
+        at = pl.ds(pl.multiple_of(e * slots, 16), slots)
+        for plane in (0, 1):
+            y_ref[plane, at, :] = y[plane * slots : (plane + 1) * slots]
+
+    @pl.when(step == local * splits - 1)
+    def _():
+        far = far_out.shape[0]
+        for plane, refs_at in enumerate(([(mine_out, 0)], [(far_out, 0), (other_out, far)])):
+            total = jnp.dot(hot_ref[plane], y_ref[plane], preferred_element_type=F32).astype(BF16)
+            width = total.shape[1]
+            for ref, at in refs_at:
+                ref[:, :width] = total[at : at + ref.shape[0]]
+                if ref.shape[1] > width:
+                    fill = (ref.shape[0], ref.shape[1] - width)
+                    ref[:, width:] = jnp.zeros(fill, BF16)
+
+
+def run_chunk(base, info, pieces, gate_up, down_t, later=()):
+    senders, fields, each = info.shape
+    count = senders // 2
+    local, _, width, units = gate_up.shape
+    splits = 2
+    slots = count * CAP
+    unit = units // splits
+    wide = pieces[0].shape[1]
+    whole = [pl.BlockSpec(p.shape, lambda i, *_: (0, 0)) for p in pieces]
+    heights = [count * each, each, (count - 1) * each]
+    macs = 2 * local * slots * width * (3 * units + 2 * count * each)
+    body = functools.partial(
+        chunk_kernel, local=local, count=count, splits=splits, held=len(pieces), passed=len(later)
+    )
+    hand_on = [pl.BlockSpec(memory_space=pl.ANY)] * len(later)
+    first_later = 4 + len(pieces)
     return pl.pallas_call(
-        functools.partial(pick_kernel, local=local),
+        body,
         grid_spec=pltpu.PrefetchScalarGridSpec(
             num_scalar_prefetch=1,
-            grid=(steps,),
+            grid=(local * splits,),
             in_specs=[
-                pl.BlockSpec((PACK, top, each), lambda i, *_: (i, 0, 0)),
-                pl.BlockSpec((PACK, top, each), lambda i, *_: (i, 0, 0)),
-                pl.BlockSpec((PACK * each, width), lambda i, *_: (i, 0)),
+                pl.BlockSpec((senders, fields, each), lambda i, *_: (0, 0, 0)),
+                *whole,
+                pl.BlockSpec((1, 2, width, unit), lambda i, *_: (i // splits, 0, 0, i % splits)),
+                pl.BlockSpec((1, width, unit), lambda i, *_: (i // splits, 0, i % splits)),
+                *hand_on,
             ],
             out_specs=[
-                pl.BlockSpec((local, slots, width), lambda i, *_: (0, i, 0)),
-                pl.BlockSpec((local, slots, 1), lambda i, *_: (0, i, 0)),
+                *[pl.BlockSpec((h, wide), lambda i, *_: (0, 0)) for h in heights],
+                *hand_on,
+            ],
+            scratch_shapes=[
+                pltpu.VMEM((local, 2 * slots, width), BF16),
+                pltpu.VMEM((local, 2 * slots, 128), F32),
+                pltpu.VMEM((2, count * each, local * slots), BF16),
+                pltpu.VMEM((2 * slots, width), F32),
+                pltpu.VMEM((2, local * slots, width), BF16),
             ],
         ),
         out_shape=[
-            jax.ShapeDtypeStruct((local, senders * CAP, width), BF16),
-            jax.ShapeDtypeStruct((local, senders * CAP, 1), F32),
+            *[jax.ShapeDtypeStruct((h, wide), BF16) for h in heights],
+            *[jax.ShapeDtypeStruct(p.shape, p.dtype) for p in later],
         ],
-        compiler_params=params(48),
+        input_output_aliases={first_later + i: 3 + i for i in range(len(later))},
+        compiler_params=params(VMEM_MIB),
         cost_estimate=pl.CostEstimate(
-            flops=2 * steps * local * slots * PACK * each * width,
-            bytes_accessed=2 * (rows.size + local * senders * CAP * width),
+            flops=2 * macs,
+            bytes_accessed=2 * (gate_up.size + down_t.size + 4 * count * each * wide),
             transcendentals=0,
         ),
-        name="pick_rows",
-    )(base, routes, weights, rows)
-
-
-def expert_kernel(x_ref, w_ref, up_ref, down_ref, y_ref):
-    x = x_ref[0]
-    gate = jnp.dot(x, up_ref[0, 0], preferred_element_type=F32)
-    up = jnp.dot(x, up_ref[0, 1], preferred_element_type=F32)
-    act = ((up + 1.0) * gate * jax.nn.sigmoid(1.702 * gate)).astype(BF16)
-    out = jnp.dot(act, down_ref[0], preferred_element_type=F32)
-    y_ref[0] = (out * w_ref[0]).astype(BF16)
-
-
-def run_experts(x, w, gate_up, down_proj, block):
-    local, slots, width = x.shape
-    units = down_proj.shape[1]
-    return pl.pallas_call(
-        expert_kernel,
-        grid=(local, slots // block),
-        in_specs=[
-            pl.BlockSpec((1, block, width), lambda e, i: (e, i, 0)),
-            pl.BlockSpec((1, block, 1), lambda e, i: (e, i, 0)),
-            pl.BlockSpec((1, 2, width, units), lambda e, i: (e, 0, 0, 0)),
-            pl.BlockSpec((1, units, width), lambda e, i: (e, 0, 0)),
-        ],
-        out_specs=pl.BlockSpec((1, block, width), lambda e, i: (e, i, 0)),
-        out_shape=jax.ShapeDtypeStruct(x.shape, BF16),
-        compiler_params=params(56),
-        cost_estimate=pl.CostEstimate(
-            flops=2 * 3 * local * slots * width * units,
-            bytes_accessed=2 * (2 * x.size + gate_up.size + down_proj.size),
-            transcendentals=local * slots * units,
-        ),
-        name="experts",
-    )(x, w, gate_up, down_proj)
-
-
-def spread_kernel(base_s, routes_ref, y_ref, out_ref, *, local):
-    rows = routes_ref.shape[1]
-    slots = PACK * CAP
-    lower = (
-        lax.broadcasted_iota(jnp.int32, (rows, rows), 1)
-        <= lax.broadcasted_iota(jnp.int32, (rows, rows), 0)
-    ).astype(F32).astype(BF16)
-    place = lax.broadcasted_iota(jnp.int32, (1, slots), 1)
-    y = y_ref[...].reshape(local * slots, y_ref.shape[2])
-    hots = []
-    for s in range(PACK):
-        route = routes_ref[s]
-        want = place - s * CAP
-        pieces = []
-        for e in range(local):
-            hit = jnp.where(route == base_s[0] + e, 1.0, 0.0)
-            member = jnp.max(hit, axis=1, keepdims=True)
-            wide = jnp.broadcast_to(member, (rows, 128)).astype(BF16)
-            counts = jnp.dot(lower, wide, preferred_element_type=F32)[:, :slots]
-            rank = jnp.where(member > 0.0, counts - 1.0, -1000.0).astype(jnp.int32)
-            pieces.append(jnp.where(rank == want, 1.0, 0.0))
-        hots.append(jnp.concatenate(pieces, axis=1).astype(BF16))
-    hot = jnp.concatenate(hots, axis=0)
-    out_ref[...] = jnp.dot(hot, y, preferred_element_type=F32).astype(BF16)
-
-
-def spread_rows(base, routes, y):
-    senders, each, top = routes.shape
-    local, _, width = y.shape
-    slots = PACK * CAP
-    steps = senders // PACK
-    return pl.pallas_call(
-        functools.partial(spread_kernel, local=local),
-        grid_spec=pltpu.PrefetchScalarGridSpec(
-            num_scalar_prefetch=1,
-            grid=(steps,),
-            in_specs=[
-                pl.BlockSpec((PACK, each, top), lambda i, *_: (i, 0, 0)),
-                pl.BlockSpec((local, slots, width), lambda i, *_: (0, i, 0)),
-            ],
-            out_specs=pl.BlockSpec((PACK * each, width), lambda i, *_: (i, 0)),
-        ),
-        out_shape=jax.ShapeDtypeStruct((senders * each, width), BF16),
-        compiler_params=params(48),
-        cost_estimate=pl.CostEstimate(
-            flops=2 * steps * local * slots * PACK * each * width,
-            bytes_accessed=2 * (y.size + senders * each * width),
-            transcendentals=0,
-        ),
-        name="spread_rows",
-    )(base, routes, y)
+        name="chunk",
+    )(base, info, *pieces, gate_up, down_t, *later)
 
 
 def exchange(value, axes, count, step):
     return lax.ppermute(value, axes, [(i, i ^ step) for i in range(count)])
+
+
+def add(a, b):
+    return (a.astype(F32) + b.astype(F32)).astype(BF16)
 
 
 def attention_and_norm(
@@ -327,8 +351,19 @@
     terms = []
     for step in order:
         term = jnp.dot(arrived[step], out_proj, preferred_element_type=F32).astype(BF16)
+        term = jnp.swapaxes(term, 0, 1)
         terms.append(exchange(term, dp, dp_count, step) if step else term)
-    return mix_and_norm(hidden_in, terms, norm_gain)
+    return mix_and_norm(jnp.swapaxes(hidden_in, 0, 1), terms, norm_gain)
+
+
+def second_hop(mine, other, a_xy, b_xy, to):
+    half = a_xy.shape[0]
+    each = 2 * half
+    for_x = add(mine[each : 2 * each], other[:each])
+    for_y = add(mine[2 * each : 3 * each], other[each : 2 * each])
+    for_x = jnp.concatenate([add(for_x[:half], a_xy), for_x[half:]], axis=0)
+    for_y = jnp.concatenate([for_y[:half], add(for_y[half:], b_xy)], axis=0)
+    return to(for_x, "x"), to(for_y, "y")
 
 
 def layer_gathered(
@@ -336,34 +371,59 @@
     routes, route_weights, gate_up, down_proj, *, sizes,
 ):
     ny, nx, nz, nc = sizes
-    everyone = ("y", "x", "z", "core")
-    each, top = routes.shape
     local = gate_up.shape[0]
+    half = hidden_in.shape[0] // 2
     base = ((lax.axis_index("z") * nc + lax.axis_index("core")) * local).astype(jnp.int32)
     base = base.reshape(1)
 
-    def by_core(info):
-        info = lax.all_gather(info, everyone, axis=0, tiled=False)
-        info = info.reshape((ny * nx * nz, nc) + info.shape[1:])
-        return jnp.swapaxes(info, 0, 1).reshape((ny * nx * nz * nc,) + info.shape[2:])
-
-    all_routes = by_core(routes)
-    all_routes_t = jnp.swapaxes(all_routes, 1, 2)
-    all_weights_t = jnp.swapaxes(by_core(route_weights), 1, 2)
+    def to(value, axis, step=1):
+        return exchange(value, axis, nz if axis == "z" else 2, step)
+
+    info = jnp.concatenate([routes.astype(F32), route_weights], axis=1)
+    info = jnp.swapaxes(info, 0, 1)[None]
+    for axis, step in (("x", 1), ("y", 1), ("core", 1), ("z", 1), ("z", 2)):
+        info = jnp.concatenate([info, to(info, axis, step)], axis=0)
+    info = info.reshape((nz, ny * nx * nc) + info.shape[1:])
+
     mixed, normed = attention_and_norm(
         hidden_in, queries, kv_pages, page_table, new_rows, context, sink_logits, out_proj,
         norm_gain, ("y", "x"), ny * nx,
     )
-    rows = lax.all_gather(normed, "z", axis=0, tiled=True)
-    rows = lax.all_gather(rows, ("y", "x"), axis=0, tiled=True)
-    rows = lax.all_gather(rows, "core", axis=0, tiled=True)
-    x, w = pick_rows(base, all_routes_t, all_weights_t, rows, local)
-    y = run_experts(x, w, gate_up, down_proj, x.shape[1] // 2)
-    total = spread_rows(base, all_routes, y)
-    total = lax.psum_scatter(total, "core", scatter_dimension=0, tiled=True)
-    total = lax.psum_scatter(total, ("y", "x"), scatter_dimension=0, tiled=True)
-    total = lax.psum_scatter(total, "z", scatter_dimension=0, tiled=True)
-    return (mixed.astype(F32) + total.astype(F32)).astype(BF16)
+    down_t = jnp.swapaxes(down_proj, 1, 2)
+    rows = {0: normed, 1: to(normed, "z", 1), 2: to(normed, "z", 2)}
+    rows[3] = to(rows[2], "z", 1)
+    each = 2 * half
+    order = (0, 2, 3, 1)
+    sums, held, came = {}, {}, {}
+    for at, r in enumerate(order):
+        own = rows[r]
+        own_x, own_y = to(own, "x"), to(own, "y")
+        pieces = [own, own_x, own_y, to(own_x[:half], "y"), to(own_y[half:], "x")]
+        pieces += [to(piece, "core") for piece in pieces]
+        later = {("row", n): rows[n] for n in order[at + 2 : at + 3]}
+        later.update({("far", n): held[n][2:] for n in order[at - 2 : at - 1] if at > 1})
+        flat, tree = jax.tree.flatten(later)
+        mine, far, other, *flat = run_chunk(base, info[r], pieces, gate_up, down_t, flat)
+        later = jax.tree.unflatten(tree, flat)
+        for (what, n), value in later.items():
+            if what == "row":
+                rows[n] = value
+            elif what == "far":
+                came[n] = second_hop(held[n][0], held[n][1], *value, to)
+            else:
+                came[n] = value
+        far, other = to(far, "core"), to(other, "core")
+        far = add(mine[:each], far)
+        held[r] = (mine, other, to(far[:half], "y"), to(far[half:], "x"))
+    for r in order[2:]:
+        came[r] = second_hop(*held[r], to)
+    for r in order:
+        mine, other = held[r][:2]
+        kept = add(mine[3 * each :], other[2 * each :])
+        sums[r] = add(add(kept, came[r][0]), came[r][1])
+        if r:
+            sums[r] = to(sums[r], "z", r)
+    return jnp.swapaxes(finish(mixed, [sums[r] for r in range(nz)]), 0, 1)
 
 
 def layer_sent(
@@ -375,6 +435,8 @@
         hidden_in, queries, kv_pages, page_table, new_rows, context, sink_logits, out_proj,
         norm_gain, "dp", dp_count,
     )
+    mixed = jnp.swapaxes(mixed, 0, 1)
+    normed = normed[:, :model_width]
     assign = routes.reshape(-1)
     onehot = (assign[:, None] == jnp.arange(E, dtype=jnp.int32)[None, :]).astype(jnp.int32)
     slot_index = jnp.sum((jnp.cumsum(onehot, axis=0) - onehot) * onehot, axis=1)

time: 677 us -> 470 us (0.69)
  waiting for transfers between devices: 410 us -> 190 us
  blocking collectives: 77.6 us -> 0 us
  starting transfers between devices: 8.44 us -> 62.3 us
  Pallas kernels: 117 us -> 163 us
  local copies, waits for them, and re-layouts: 40.1 us -> 12.9 us
  other arithmetic: 1.3 us -> 20.8 us
  between operations: 13.7 us -> 1.3 us
    reduce_scatter x2 -> x0, waiting for transfers between devices: 181 us -> none  [the longest x1 121 us: layer_gathered(): total = lax.psum_scatter(total, ('y', 'x'), scatter_dimension=0, tiled=True)]
    all_gather x3 -> x0, waiting for transfers between devices: 180 us -> none  [the longest x1 119 us: layer_gathered(): rows = lax.all_gather(rows, ('y', 'x'), axis=0, tiled=True)]
    ppermute x6 -> x77, waiting for transfers between devices: 16 us -> 190 us  [exchange(): return lax.ppermute(value, axes, [(i, i ^ step) for i in range(count)])]
    all_gather x2 -> x0, blocking collectives: 77.6 us -> none  [by_core(): info = lax.all_gather(info, everyone, axis=0, tiled=False)]
    ppermute x6 -> x77, starting transfers between devices: 8.24 us -> 62.3 us  [exchange(): return lax.ppermute(value, axes, [(i, i ^ step) for i in range(count)])]
    pallas_call x4 -> x6, Pallas kernels: 81.1 us -> 119 us  [the longest x4 111 us: run_chunk(): pl.pallas_call(body, grid_spec=pltpu.PrefetchScalarGridSpec(num_scalar_pr...]
    unnamed x7 -> x0, waiting for transfers between devices: 32.7 us -> none
    unnamed x44 -> x111, local copies, waits for them, and re-layouts: 31.1 us -> 3.1 us
  transfers between devices with their start and end apart: 12 -> 77, of which waited for: 8 -> 22; matrix products, arithmetic and copies ran while one was open for 4% -> 9% of each run, Pallas kernels for 4% -> 31%
where the time goes in v2:
time: 470 us; the launch traced here: 463 us
  waiting for transfers between devices  190 us (40%)
  Pallas kernels  163 us (35%)
  starting transfers between devices  62.3 us (13%)
  other arithmetic  20.8 us (4%)
  local copies, waits for them, and re-layouts  12.9 us (3%)
  matrix products  12.2 us (3%)
    ppermute x77, waiting for transfers between devices, exchange(): return lax.ppermute(value, axes, [(i, i ^ step) for i in range(count)])  190 us
    pallas_call x4, Pallas kernels, run_chunk(): pl.pallas_call(body, grid_spec=pltpu.PrefetchScalarGridSpec(num_scalar_pr...  111 us
    ppermute x77, starting transfers between devices, exchange(): return lax.ppermute(value, axes, [(i, i ^ step) for i in range(count)])  62.3 us
    pallas_call x4, Pallas kernels, attend_group(): pl.pallas_call(body, grid_spec=pltpu.PrefetchScalarGridSpec(num_scalar_pr...  43.9 us
    convert_element_type x16, other arithmetic, add(): return (a.astype(F32) + b.astype(F32)).astype(BF16)  18.5 us
    dot_general x4, matrix products, attention_and_norm(): jnp.dot(arrived[step], out_proj, preferred_element_type=F32).astype(BF16)  12.2 us
  transfers between devices with their start and end apart: 77, of which 22 were waited for; matrix products, arithmetic and copies ran while one was open for 9% of the time, Pallas kernels for 31%

profile of v2, /device:TPU:0, one launch (start us, length us, event | category | flops | bytes accessed | tf_op | source)
XLA Modules:
  0.0 462.6 jit_solution(4907640304589057750)
XLA Ops:
  1.3 10.8 %attend.4 = bf16[128,1024]{1,0:T(8,128)(2,1)} custom-call(s32[1]{0:T(128)} %bitcast.1.col_s, s32[4]{0:T(128)} %rows_s.7, s32[4]{0:T(128)} %ctx_s.7, s32[16]{0:T(128)} %reshape.34.table_s, f32[64]{0:T(128)} %sink_s.7, bf16[128,4096]{1,0:T(8,128)(2,1)} %q_ref.7, bf16[16,128,1024]{2,1,0:T(8,128)(2,1)} %kv_ref.7), custom_call_target="tpu_custom_call" | custom-call | flops 2147483648 | bytes 1572864 | tf_op jit(solution)/shard_map/attend/pallas_call | solution.py:104
  12.1 3.9 collective-permute-start
  16.0 11.0 %attend.5 = bf16[128,1024]{1,0:T(8,128)(2,1)} custom-call(s32[1]{0:T(128)} %bitcast.3.col_s, s32[4]{0:T(128)} %rows_s.7, s32[4]{0:T(128)} %ctx_s.7, s32[16]{0:T(128)} %reshape.34.table_s, f32[64]{0:T(128)} %sink_s.7, bf16[128,4096]{1,0:T(8,128)(2,1)} %q_ref.7, bf16[16,128,1024]{2,1,0:T(8,128)(2,1)} %kv_ref.7), custom_call_target="tpu_custom_call" | custom-call | flops 2147483648 | bytes 1572864 | tf_op jit(solution)/shard_map/attend/pallas_call | solution.py:104
  27.5 11.4 %attend.6 = bf16[128,1024]{1,0:T(8,128)(2,1)} custom-call(s32[1]{0:T(128)} %bitcast.5.col_s, s32[4]{0:T(128)} %rows_s.7, s32[4]{0:T(128)} %ctx_s.7, s32[16]{0:T(128)} %reshape.34.table_s, f32[64]{0:T(128)} %sink_s.7, bf16[128,4096]{1,0:T(8,128)(2,1)} %q_ref.7, bf16[16,128,1024]{2,1,0:T(8,128)(2,1)} %kv_ref.7), custom_call_target="tpu_custom_call" | custom-call | flops 2147483648 | bytes 1572864 | tf_op jit(solution)/shard_map/attend/pallas_call | solution.py:104
  38.9 3.5 fusion
  42.4 2.9 collective-permute-start.1
  45.4 2.6 fusion.1
  48.4 2.6 fusion.2
  51.7 10.8 %attend.7 = bf16[128,1024]{1,0:T(8,128)(2,1)} custom-call(s32[1]{0:T(128)} %bitcast.7.col_s, s32[4]{0:T(128)} %rows_s.7, s32[4]{0:T(128)} %ctx_s.7, s32[16]{0:T(128)} %reshape.34.table_s, f32[64]{0:T(128)} %sink_s.7, bf16[128,4096]{1,0:T(8,128)(2,1)} %q_ref.7, bf16[16,128,1024]{2,1,0:T(8,128)(2,1)} %kv_ref.7), custom_call_target="tpu_custom_call" | custom-call | flops 2147483648 | bytes 1572864 | tf_op jit(solution)/shard_map/attend/pallas_call | solution.py:104
  62.5 3.5 fusion.3.d_ref
  66.1 13.1 %collective-permute-done.3.b_ref = bf16[2880,128]{1,0:T(8,128)(2,1)} collective-permute-done((bf16[2880,128]{1,0:T(8,128)(2,1)}, bf16[2880,128]{1,0:T(8,128)(2,1)}, u32[]{:S(2)}, u32[]{:S(2)}) %collective-permute-start.3) | collective-permute-done | bytes 737312 | tf_op jit(solution)/shard_map/ppermute | solution.py:331
  79.2 4.7 %mix_norm.1 = (bf16[2880,128]{1,0:T(8,128)(2,1)}, bf16[128,2944]{1,0:T(8,128)(2,1)}) custom-call(bf16[2880,128]{1,0:T(8,128)(2,1)} %bitcast.36, bf16[2880,128]{1,0:T(8,128)(2,1)} %collective-permute-done.1.a_ref, bf16[2880,128]{1,0:T(8,128)(2,1)} %collective-permute-done.3.b_ref, bf16[2880,128]{1,0:T(8,128)(2,1)} %collective-permute-done.5.c_ref, ...), custom_call_target="tpu_custom_call" | custom-call | tf_op jit(solution)/shard_map/mix_norm/pallas_call | solution.py:145
  85.0 2.6 collective-permute-start.18
  87.7 1.6 collective-permute-start.6
  89.2 13.7 %collective-permute-done.6 = f32[1,8,128]{2,1,0:T(8,128)S(1)} collective-permute-done((f32[1,8,128]{2,1,0:T(8,128)S(1)}, f32[1,8,128]{2,1,0:T(8,128)S(1)}, u32[]{:S(2)}, u32[]{:S(2)}) %collective-permute-start.6) | collective-permute-done | bytes 4128 | tf_op jit(solution)/shard_map/ppermute | solution.py:331
  103.5 3.1 collective-permute-done.7
  108.9 12.7 %collective-permute-done.18.refs_0_ = bf16[128,2944]{1,0:T(8,128)(2,1)} collective-permute-done((bf16[128,2944]{1,0:T(8,128)(2,1)}, bf16[128,2944]{1,0:T(8,128)(2,1)}, u32[]{:S(2)}, u32[]{:S(2)}) %collective-permute-start.18) | collective-permute-done | bytes 753696 | tf_op jit(solution)/shard_map/ppermute | solution.py:331
  125.0 1.5 collective-permute-start.37
  127.9 13.7 %collective-permute-done.19.refs_12_ = bf16[128,2944]{1,0:T(8,128)(2,1)S(1)} collective-permute-done((bf16[128,2944]{1,0:T(8,128)(2,1)}, bf16[128,2944]{1,0:T(8,128)(2,1)S(1)}, u32[]{:S(2)}, u32[]{:S(2)}) %collective-permute-start.19) | collective-permute-done | bytes 753696 | tf_op jit(solution)/shard_map/ppermute | solution.py:331
  142.5 27.9 %chunk.4 = (bf16[512,2944]{1,0:T(8,128)(2,1)}, bf16[128,2944]{1,0:T(8,128)(2,1)}, bf16[384,2944]{1,0:T(8,128)(2,1)}, bf16[128,2944]{1,0:T(8,128)(2,1)}) custom-call(s32[1]{0:T(128)} %bitcast.9.base_s, f32[8,8,128]{2,1,0:T(8,128)} %copy-done.47, bf16[128,2944]{1,0:T(8,128)(2,1)} %get-tuple-element.26.refs_0_, ...), custom_call_target="tpu_custom_call", output_to_operand_aliasing={{3}: (14, {})} | custom-call | flops 9437184000 | bytes 47448064 | tf_op jit(solution)/shard_map/chunk/pallas_call | solution.py:291
  170.6 2.0 collective-permute-start.22
  173.0 4.5 collective-permute-done.22
  180.4 8.3 %collective-permute-done.39.refs_3_ = bf16[64,2944]{1,0:T(8,128)(2,1)S(1)} collective-permute-done((bf16[64,2944]{1,0:T(8,128)(2,1)S(1)}, bf16[64,2944]{1,0:T(8,128)(2,1)S(1)}, u32[]{:S(2)}, u32[]{:S(2)}) %collective-permute-start.39) | collective-permute-done | bytes 376864 | tf_op jit(solution)/shard_map/ppermute | solution.py:331
  190.5 1.5 collective-permute-start.23
  193.7 27.6 %chunk.6 = (bf16[512,2944]{1,0:T(8,128)(2,1)}, bf16[128,2944]{1,0:T(8,128)(2,1)}, bf16[384,2944]{1,0:T(8,128)(2,1)}, bf16[128,2944]{1,0:T(8,128)(2,1)}) custom-call(s32[1]{0:T(128)} %bitcast.9.base_s, f32[8,8,128]{2,1,0:T(8,128)} %get-tuple-element.65.info_ref, bf16[128,2944]{1,0:T(8,128)(2,1)} %collective-permute-done.18.refs_0_, ...), custom_call_target="tpu_custom_call", output_to_operand_aliasing={{3}: (14, {})} | custom-call | flops 9437184000 | bytes 47448064 | tf_op jit(solution)/shard_map/chunk/pallas_call | solution.py:291
  226.2 2.2 add_convert_fusion.22
  228.5 1.5 collective-permute-start.26
  230.0 20.2 %collective-permute-done.25.refs_3_ = bf16[64,2944]{1,0:T(8,128)(2,1)S(1)} collective-permute-done((bf16[64,2944]{1,0:T(8,128)(2,1)S(1)}, bf16[64,2944]{1,0:T(8,128)(2,1)S(1)}, u32[]{:S(2)}, u32[]{:S(2)}) %collective-permute-start.25) | collective-permute-done | bytes 376864 | tf_op jit(solution)/shard_map/ppermute | solution.py:331
  257.6 4.5 collective-permute-done.33.refs_12_
  264.8 27.8 %chunk.5 = (bf16[512,2944]{1,0:T(8,128)(2,1)}, bf16[128,2944]{1,0:T(8,128)(2,1)}, bf16[384,2944]{1,0:T(8,128)(2,1)}, bf16[64,2944]{1,0:T(8,128)(2,1)}, bf16[64,2944]{1,0:T(8,128)(2,1)}) custom-call(s32[1]{0:T(128)} %bitcast.9.base_s, f32[8,8,128]{2,1,0:T(8,128)} %get-tuple-element.66.info_ref, ...), custom_call_target="tpu_custom_call", output_to_operand_aliasing={{3}: (14, {}), {4}: (15, {})} | custom-call | flops 9437184000 | bytes 47448064 | tf_op jit(solution)/shard_map/chunk/pallas_call | solution.py:291
  296.3 2.1 add_convert_fusion.9
  307.0 3.3 collective-permute-done.57.refs_12_
  311.1 27.7 %chunk.7 = (bf16[512,2944]{1,0:T(8,128)(2,1)}, bf16[128,2944]{1,0:T(8,128)(2,1)}, bf16[384,2944]{1,0:T(8,128)(2,1)}, bf16[64,2944]{1,0:T(8,128)(2,1)}, bf16[64,2944]{1,0:T(8,128)(2,1)}) custom-call(s32[1]{0:T(128)} %bitcast.9.base_s, f32[8,8,128]{2,1,0:T(8,128)} %copy-done.46, ...), custom_call_target="tpu_custom_call", output_to_operand_aliasing={{3}: (14, {}), {4}: (15, {})} | custom-call | flops 9437184000 | bytes 47448064 | tf_op jit(solution)/shard_map/chunk/pallas_call | solution.py:291
  343.6 2.1 add_convert_fusion.4
  345.8 15.0 %collective-permute-done.68 = bf16[128,2944]{1,0:T(8,128)(2,1)S(1)} collective-permute-done((bf16[128,2944]{1,0:T(8,128)(2,1)S(1)}, bf16[128,2944]{1,0:T(8,128)(2,1)S(1)}, u32[]{:S(2)}, u32[]{:S(2)}) %collective-permute-start.68) | collective-permute-done | bytes 753696 | tf_op jit(solution)/shard_map/ppermute | solution.py:331
  364.1 7.9 %collective-permute-done.74 = bf16[64,2944]{1,0:T(8,128)(2,1)S(1)} collective-permute-done((bf16[64,2944]{1,0:T(8,128)(2,1)S(1)}, bf16[64,2944]{1,0:T(8,128)(2,1)S(1)}, u32[]{:S(2)}, u32[]{:S(2)}) %collective-permute-start.74) | collective-permute-done | bytes 376864 | tf_op jit(solution)/shard_map/ppermute | solution.py:331
  375.6 9.1 %collective-permute-done.72 = bf16[64,2944]{1,0:T(8,128)(2,1)S(1)} collective-permute-done((bf16[64,2944]{1,0:T(8,128)(2,1)S(1)}, bf16[64,2944]{1,0:T(8,128)(2,1)S(1)}, u32[]{:S(2)}, u32[]{:S(2)}) %collective-permute-start.72) | collective-permute-done | bytes 376864 | tf_op jit(solution)/shard_map/ppermute | solution.py:331
  385.6 6.7 %collective-permute-done.63 = bf16[64,2944]{1,0:T(8,128)(2,1)S(1)} collective-permute-done((bf16[64,2944]{1,0:T(8,128)(2,1)S(1)}, bf16[64,2944]{1,0:T(8,128)(2,1)S(1)}, u32[]{:S(2)}, u32[]{:S(2)}) %collective-permute-start.63) | collective-permute-done | bytes 376864 | tf_op jit(solution)/shard_map/ppermute | solution.py:331
  393.6 12.7 %collective-permute-done.61 = bf16[64,2944]{1,0:T(8,128)(2,1)S(1)} collective-permute-done((bf16[64,2944]{1,0:T(8,128)(2,1)S(1)}, bf16[64,2944]{1,0:T(8,128)(2,1)S(1)}, u32[]{:S(2)}, u32[]{:S(2)}) %collective-permute-start.61) | collective-permute-done | bytes 376864 | tf_op jit(solution)/shard_map/ppermute | solution.py:331
  407.2 1.8 collective-permute-start.64
  409.0 14.3 %collective-permute-done.73 = bf16[128,2944]{1,0:T(8,128)(2,1)S(1)} collective-permute-done((bf16[128,2944]{1,0:T(8,128)(2,1)S(1)}, bf16[128,2944]{1,0:T(8,128)(2,1)S(1)}, u32[]{:S(2)}, u32[]{:S(2)}) %collective-permute-start.73) | collective-permute-done | bytes 753696 | tf_op jit(solution)/shard_map/ppermute | solution.py:331
  424.0 1.5 add_convert_fusion
  425.5 2.6 collective-permute-start.76
  428.1 10.7 %collective-permute-done.62 = bf16[128,2944]{1,0:T(8,128)(2,1)S(1)} collective-permute-done((bf16[128,2944]{1,0:T(8,128)(2,1)S(1)}, bf16[128,2944]{1,0:T(8,128)(2,1)S(1)}, u32[]{:S(2)}, u32[]{:S(2)}) %collective-permute-start.62) | collective-permute-done | bytes 753696 | tf_op jit(solution)/shard_map/ppermute | solution.py:331
  439.1 2.8 collective-permute-start.65
  442.0 2.8 add_convert_fusion.18.refs_0_
  444.8 13.1 %collective-permute-done.65.refs_1_ = bf16[128,2944]{1,0:T(8,128)(2,1)S(1)} collective-permute-done((bf16[128,2944]{1,0:T(8,128)(2,1)S(1)}, bf16[128,2944]{1,0:T(8,128)(2,1)S(1)}, u32[]{:S(2)}, u32[]{:S(2)}) %collective-permute-start.65) | collective-permute-done | bytes 753696 | tf_op jit(solution)/shard_map/ppermute | solution.py:331
  458.8 3.4 finish.1
  (286 shorter events, 63.8 us)
Async XLA Ops:
  12.1 26.8 %collective-permute-start = (bf16[128,1024]{1,0:T(8,128)(2,1)}, bf16[128,1024]{1,0:T(8,128)(2,1)}, u32[]{:S(2)}, u32[]{:S(2)}) collective-permute-start(bf16[128,1024]{1,0:T(8,128)(2,1)} %attend.4), channel_id=1, source_target_pairs={{0,24},{8,16},{16,8},{24,0},{1,25},{9,17},{17,9},{25,1},{2,26},{10... | collective-permute-start | bytes 786440 | tf_op jit(solution)/shard_map/ppermute | solution.py:331
  27.0 18.4 %collective-permute-start.2 = (bf16[128,1024]{1,0:T(8,128)(2,1)}, bf16[128,1024]{1,0:T(8,128)(2,1)S(1)}, u32[]{:S(2)}, u32[]{:S(2)}) collective-permute-start(bf16[128,1024]{1,0:T(8,128)(2,1)} %attend.5), channel_id=1, source_target_pairs={{0,16},{8,24},{16,0},{24,8},{1,17},{9,25},{17,1},{25,9},{2,18},{10... | collective-permute-start | bytes 786440 | tf_op jit(solution)/shard_map/ppermute | solution.py:331
  42.4 23.6 %collective-permute-start.1 = (bf16[2880,128]{1,0:T(8,128)(2,1)}, bf16[2880,128]{1,0:T(8,128)(2,1)}, u32[]{:S(2)}, u32[]{:S(2)}) collective-permute-start(bf16[2880,128]{1,0:T(8,128)(2,1)} %fusion), channel_id=1, source_target_pairs={{0,24},{8,16},{16,8},{24,0},{1,25},{9,17},{17,9},{25,1},{2,26},{10... | collective-permute-start | bytes 2211848 | tf_op jit(solution)/shard_map/ppermute | solution.py:331
  47.9 31.2 %collective-permute-start.3 = (bf16[2880,128]{1,0:T(8,128)(2,1)}, bf16[2880,128]{1,0:T(8,128)(2,1)}, u32[]{:S(2)}, u32[]{:S(2)}) collective-permute-start(bf16[2880,128]{1,0:T(8,128)(2,1)} %fusion.1), channel_id=1, source_target_pairs={{0,16},{8,24},{16,0},{24,8},{1,17},{9,25},{17,1},{25,9},{2,18},{10... | collective-permute-start | bytes 2211848 | tf_op jit(solution)/shard_map/ppermute | solution.py:331
  51.1 28.1 %collective-permute-start.5 = (bf16[2880,128]{1,0:T(8,128)(2,1)}, bf16[2880,128]{1,0:T(8,128)(2,1)}, u32[]{:S(2)}, u32[]{:S(2)}) collective-permute-start(bf16[2880,128]{1,0:T(8,128)(2,1)} %fusion.2), channel_id=1, source_target_pairs={{0,8},{8,0},{16,24},{24,16},{1,9},{9,1},{17,25},{25,17},{2,10},{10... | collective-permute-start | bytes 2211848 | tf_op jit(solution)/shard_map/ppermute | solution.py:331
  83.9 22.7 %collective-permute-start.9 = (bf16[128,2944]{1,0:T(8,128)(2,1)}, bf16[128,2944]{1,0:T(8,128)(2,1)S(1)}, u32[]{:S(2)}, u32[]{:S(2)}) collective-permute-start(bf16[128,2944]{1,0:T(8,128)(2,1)} %get-tuple-element.26.refs_0_), channel_id=1, source_target_pairs={{0,8},{8,0},{1,9},{9,1},{2,10},{10,2},{3,11},{11,3},{4,12},{12,4},... | collective-permute-start | bytes 2261000 | tf_op jit(solution)/shard_map/ppermute | solution.py:331
  84.4 22.8 %collective-permute-start.10 = (bf16[128,2944]{1,0:T(8,128)(2,1)}, bf16[128,2944]{1,0:T(8,128)(2,1)S(1)}, u32[]{:S(2)}, u32[]{:S(2)}) collective-permute-start(bf16[128,2944]{1,0:T(8,128)(2,1)} %get-tuple-element.26.refs_0_), channel_id=1, source_target_pairs={{0,16},{16,0},{1,17},{17,1},{2,18},{18,2},{3,19},{19,3},{4,20},{20... | collective-permute-start | bytes 2261000 | tf_op jit(solution)/shard_map/ppermute | solution.py:331
  85.0 23.3 %collective-permute-start.13 = (bf16[128,2944]{1,0:T(8,128)(2,1)}, bf16[128,2944]{1,0:T(8,128)(2,1)S(1)}, u32[]{:S(2)}, u32[]{:S(2)}) collective-permute-start(bf16[128,2944]{1,0:T(8,128)(2,1)} %get-tuple-element.26.refs_0_), channel_id=1, source_target_pairs={{0,1},{1,0},{2,3},{3,2},{4,5},{5,4},{6,7},{7,6},{8,9},{9,8},{10,11... | collective-permute-start | bytes 2261000 | tf_op jit(solution)/shard_map/ppermute | solution.py:331
  85.0 36.6 %collective-permute-start.18 = (bf16[128,2944]{1,0:T(8,128)(2,1)}, bf16[128,2944]{1,0:T(8,128)(2,1)}, u32[]{:S(2)}, u32[]{:S(2)}) collective-permute-start(bf16[128,2944]{1,0:T(8,128)(2,1)} %get-tuple-element.26.refs_0_), channel_id=1, source_target_pairs={{0,4},{2,6},{4,0},{6,2},{1,5},{3,7},{5,1},{7,3},{8,12},{10,14},{12... | collective-permute-start | bytes 2261000 | tf_op jit(solution)/shard_map/ppermute | solution.py:331
  87.7 15.3 %collective-permute-start.6 = (f32[1,8,128]{2,1,0:T(8,128)S(1)}, f32[1,8,128]{2,1,0:T(8,128)S(1)}, u32[]{:S(2)}, u32[]{:S(2)}) collective-permute-start(f32[1,8,128]{2,1,0:T(8,128)S(1)} %maximum_bitcast_fusion), channel_id=1, source_target_pairs={{0,8},{8,0},{1,9},{9,1},{2,10},{10,2},{3,11},{11,3},{4,12},{12,4},... | collective-permute-start | bytes 12296 | tf_op jit(solution)/shard_map/ppermute | solution.py:331
  106.7 16.2 %collective-permute-start.14 = (bf16[128,2944]{1,0:T(8,128)(2,1)S(1)}, bf16[128,2944]{1,0:T(8,128)(2,1)}, u32[]{:S(2)}, u32[]{:S(2)}) collective-permute-start(bf16[128,2944]{1,0:T(8,128)(2,1)S(1)} %collective-permute-done.9.refs_1_), channel_id=1, source_target_pairs={{0,1},{1,0},{2,3},{3,2},{4,5},{5,4},{6,7},{7,6},{8,9},{9,8},{10,11... | collective-permute-start | bytes 2261000 | tf_op jit(solution)/shard_map/ppermute | solution.py:331
  107.3 17.0 %collective-permute-start.15 = (bf16[128,2944]{1,0:T(8,128)(2,1)S(1)}, bf16[128,2944]{1,0:T(8,128)(2,1)}, u32[]{:S(2)}, u32[]{:S(2)}) collective-permute-start(bf16[128,2944]{1,0:T(8,128)(2,1)S(1)} %collective-permute-done.10.refs_2_), channel_id=1, source_target_pairs={{0,1},{1,0},{2,3},{3,2},{4,5},{5,4},{6,7},{7,6},{8,9},{9,8},{10,11... | collective-permute-start | bytes 2261000 | tf_op jit(solution)/shard_map/ppermute | solution.py:331
  121.7 20.0 %collective-permute-start.19 = (bf16[128,2944]{1,0:T(8,128)(2,1)}, bf16[128,2944]{1,0:T(8,128)(2,1)S(1)}, u32[]{:S(2)}, u32[]{:S(2)}) collective-permute-start(bf16[128,2944]{1,0:T(8,128)(2,1)} %collective-permute-done.18.refs_0_), channel_id=1, source_target_pairs={{0,2},{2,0},{4,6},{6,4},{1,3},{3,1},{5,7},{7,5},{8,10},{10,8},{12,... | collective-permute-start | bytes 2261000 | tf_op jit(solution)/shard_map/ppermute | solution.py:331
  122.9 47.5 %collective-permute-start.21 = (f32[8,8,128]{2,1,0:T(8,128)S(1)}, f32[8,8,128]{2,1,0:T(8,128)S(1)}, u32[]{:S(2)}, u32[]{:S(2)}) collective-permute-start(f32[8,8,128]{2,1,0:T(8,128)S(1)} %pad_maximum_fusion.8.info_ref), channel_id=1, source_target_pairs={{0,2},{2,0},{4,6},{6,4},{1,3},{3,1},{5,7},{7,5},{8,10},{10,8},{12,... | collective-permute-start | bytes 98312 | tf_op jit(solution)/shard_map/ppermute | solution.py:331
  124.3 53.2 %collective-permute-start.46 = (bf16[128,2944]{1,0:T(8,128)(2,1)}, bf16[128,2944]{1,0:T(8,128)(2,1)}, u32[]{:S(2)}, u32[]{:S(2)}) collective-permute-start(bf16[128,2944]{1,0:T(8,128)(2,1)} %get-tuple-element.26.refs_0_), channel_id=1, source_target_pairs={{0,2},{2,0},{4,6},{6,4},{1,3},{3,1},{5,7},{7,5},{8,10},{10,8},{12,... | collective-permute-start | bytes 2261000 | tf_op jit(solution)/shard_map/ppermute | solution.py:331
  125.0 45.6 %collective-permute-start.37 = (bf16[128,2944]{1,0:T(8,128)(2,1)}, bf16[128,2944]{1,0:T(8,128)(2,1)S(1)}, u32[]{:S(2)}, u32[]{:S(2)}) collective-permute-start(bf16[128,2944]{1,0:T(8,128)(2,1)} %collective-permute-done.18.refs_0_), channel_id=1, source_target_pairs={{0,8},{8,0},{1,9},{9,1},{2,10},{10,2},{3,11},{11,3},{4,12},{12,4},... | collective-permute-start | bytes 2261000 | tf_op jit(solution)/shard_map/ppermute | solution.py:331
  126.5 46.2 %collective-permute-start.38 = (bf16[128,2944]{1,0:T(8,128)(2,1)}, bf16[128,2944]{1,0:T(8,128)(2,1)S(1)}, u32[]{:S(2)}, u32[]{:S(2)}) collective-permute-start(bf16[128,2944]{1,0:T(8,128)(2,1)} %collective-permute-done.18.refs_0_), channel_id=1, source_target_pairs={{0,16},{16,0},{1,17},{17,1},{2,18},{18,2},{3,19},{19,3},{4,20},{20... | collective-permute-start | bytes 2261000 | tf_op jit(solution)/shard_map/ppermute | solution.py:331
  141.6 37.3 %collective-permute-start.41 = (bf16[128,2944]{1,0:T(8,128)(2,1)}, bf16[128,2944]{1,0:T(8,128)(2,1)S(1)}, u32[]{:S(2)}, u32[]{:S(2)}) collective-permute-start(bf16[128,2944]{1,0:T(8,128)(2,1)} %collective-permute-done.18.refs_0_), channel_id=1, source_target_pairs={{0,1},{1,0},{2,3},{3,2},{4,5},{5,4},{6,7},{7,6},{8,9},{9,8},{10,11... | collective-permute-start | bytes 2261000 | tf_op jit(solution)/shard_map/ppermute | solution.py:331
  170.4 55.7 %collective-permute-start.20 = (bf16[384,2944]{1,0:T(8,128)(2,1)}, bf16[384,2944]{1,0:T(8,128)(2,1)S(1)}, u32[]{:S(2)}, u32[]{:S(2)}) collective-permute-start(bf16[384,2944]{1,0:T(8,128)(2,1)} %get-tuple-element.28), channel_id=1, source_target_pairs={{0,1},{1,0},{2,3},{3,2},{4,5},{5,4},{6,7},{7,6},{8,9},{9,8},{10,11... | collective-permute-start | bytes 6782984 | tf_op jit(solution)/shard_map/ppermute | solution.py:331
  172.7 17.8 %collective-permute-start.42 = (bf16[128,2944]{1,0:T(8,128)(2,1)S(1)}, bf16[128,2944]{1,0:T(8,128)(2,1)S(1)}, u32[]{:S(2)}, u32[]{:S(2)}) collective-permute-start(bf16[128,2944]{1,0:T(8,128)(2,1)S(1)} %collective-permute-done.37.refs_1_), channel_id=1, source_target_pairs={{0,1},{1,0},{2,3},{3,2},{4,5},{5,4},{6,7},{7,6},{8,9},{9,8},{10,11... | collective-permute-start | bytes 2261000 | tf_op jit(solution)/shard_map/ppermute | solution.py:331
  190.5 30.8 %collective-permute-start.23 = (bf16[128,2944]{1,0:T(8,128)(2,1)S(1)}, bf16[128,2944]{1,0:T(8,128)(2,1)}, u32[]{:S(2)}, u32[]{:S(2)}) collective-permute-start(bf16[128,2944]{1,0:T(8,128)(2,1)S(1)} %copy-done.9), channel_id=1, source_target_pairs={{0,8},{8,0},{1,9},{9,1},{2,10},{10,2},{3,11},{11,3},{4,12},{12,4},... | collective-permute-start | bytes 2261000 | tf_op jit(solution)/shard_map/ppermute | solution.py:331
  192.0 31.0 %collective-permute-start.24 = (bf16[128,2944]{1,0:T(8,128)(2,1)S(1)}, bf16[128,2944]{1,0:T(8,128)(2,1)}, u32[]{:S(2)}, u32[]{:S(2)}) collective-permute-start(bf16[128,2944]{1,0:T(8,128)(2,1)S(1)} %copy-done.9), channel_id=1, source_target_pairs={{0,16},{16,0},{1,17},{17,1},{2,18},{18,2},{3,19},{19,3},{4,20},{20... | collective-permute-start | bytes 2261000 | tf_op jit(solution)/shard_map/ppermute | solution.py:331
  192.8 35.7 %collective-permute-start.27 = (bf16[128,2944]{1,0:T(8,128)(2,1)S(1)}, bf16[128,2944]{1,0:T(8,128)(2,1)}, u32[]{:S(2)}, u32[]{:S(2)}) collective-permute-start(bf16[128,2944]{1,0:T(8,128)(2,1)S(1)} %copy-done.9), channel_id=1, source_target_pairs={{0,1},{1,0},{2,3},{3,2},{4,5},{5,4},{6,7},{7,6},{8,9},{9,8},{10,11... | collective-permute-start | bytes 2261000 | tf_op jit(solution)/shard_map/ppermute | solution.py:331
  192.8 32.5 %collective-permute-start.32 = (bf16[128,2944]{1,0:T(8,128)(2,1)}, bf16[128,2944]{1,0:T(8,128)(2,1)}, u32[]{:S(2)}, u32[]{:S(2)}) collective-permute-start(bf16[128,2944]{1,0:T(8,128)(2,1)} %get-tuple-element.30), channel_id=1, source_target_pairs={{0,1},{1,0},{2,3},{3,2},{4,5},{5,4},{6,7},{7,6},{8,9},{9,8},{10,11... | collective-permute-start | bytes 2261000 | tf_op jit(solution)/shard_map/ppermute | solution.py:331
  221.3 29.6 %collective-permute-start.47 = (bf16[128,2944]{1,0:T(8,128)(2,1)}, bf16[128,2944]{1,0:T(8,128)(2,1)S(1)}, u32[]{:S(2)}, u32[]{:S(2)}) collective-permute-start(bf16[128,2944]{1,0:T(8,128)(2,1)} %get-tuple-element.33.refs_0_), channel_id=1, source_target_pairs={{0,8},{8,0},{1,9},{9,1},{2,10},{10,2},{3,11},{11,3},{4,12},{12,4},... | collective-permute-start | bytes 2261000 | tf_op jit(solution)/shard_map/ppermute | solution.py:331
  223.0 29.3 %collective-permute-start.48 = (bf16[128,2944]{1,0:T(8,128)(2,1)}, bf16[128,2944]{1,0:T(8,128)(2,1)S(1)}, u32[]{:S(2)}, u32[]{:S(2)}) collective-permute-start(bf16[128,2944]{1,0:T(8,128)(2,1)} %get-tuple-element.33.refs_0_), channel_id=1, source_target_pairs={{0,16},{16,0},{1,17},{17,1},{2,18},{18,2},{3,19},{19,3},{4,20},{20... | collective-permute-start | bytes 2261000 | tf_op jit(solution)/shard_map/ppermute | solution.py:331
  225.4 24.8 %collective-permute-start.25 = (bf16[64,2944]{1,0:T(8,128)(2,1)S(1)}, bf16[64,2944]{1,0:T(8,128)(2,1)S(1)}, u32[]{:S(2)}, u32[]{:S(2)}) collective-permute-start(bf16[64,2944]{1,0:T(8,128)(2,1)S(1)} %slice.263), channel_id=1, source_target_pairs={{0,16},{16,0},{1,17},{17,1},{2,18},{18,2},{3,19},{19,3},{4,20},{20... | collective-permute-start | bytes 1130504 | tf_op jit(solution)/shard_map/ppermute | solution.py:331
  226.2 24.6 %collective-permute-start.28 = (bf16[128,2944]{1,0:T(8,128)(2,1)}, bf16[128,2944]{1,0:T(8,128)(2,1)S(1)}, u32[]{:S(2)}, u32[]{:S(2)}) collective-permute-start(bf16[128,2944]{1,0:T(8,128)(2,1)} %collective-permute-done.23.refs_1_), channel_id=1, source_target_pairs={{0,1},{1,0},{2,3},{3,2},{4,5},{5,4},{6,7},{7,6},{8,9},{9,8},{10,11... | collective-permute-start | bytes 2261000 | tf_op jit(solution)/shard_map/ppermute | solution.py:331
  228.5 21.8 %collective-permute-start.26 = (bf16[64,2944]{1,0:T(8,128)(2,1)S(1)}, bf16[64,2944]{1,0:T(8,128)(2,1)S(1)}, u32[]{:S(2)}, u32[]{:S(2)}) collective-permute-start(bf16[64,2944]{1,0:T(8,128)(2,1)S(1)} %slice.264), channel_id=1, source_target_pairs={{0,8},{8,0},{1,9},{9,1},{2,10},{10,2},{3,11},{11,3},{4,12},{12,4},... | collective-permute-start | bytes 1130504 | tf_op jit(solution)/shard_map/ppermute | solution.py:331
  256.9 41.6 %collective-permute-start.51 = (bf16[128,2944]{1,0:T(8,128)(2,1)}, bf16[128,2944]{1,0:T(8,128)(2,1)}, u32[]{:S(2)}, u32[]{:S(2)}) collective-permute-start(bf16[128,2944]{1,0:T(8,128)(2,1)} %get-tuple-element.33.refs_0_), channel_id=1, source_target_pairs={{0,1},{1,0},{2,3},{3,2},{4,5},{5,4},{6,7},{7,6},{8,9},{9,8},{10,11... | collective-permute-start | bytes 2261000 | tf_op jit(solution)/shard_map/ppermute | solution.py:331
  257.0 38.9 %collective-permute-start.66 = (bf16[384,2944]{1,0:T(8,128)(2,1)}, bf16[384,2944]{1,0:T(8,128)(2,1)}, u32[]{:S(2)}, u32[]{:S(2)}) collective-permute-start(bf16[384,2944]{1,0:T(8,128)(2,1)} %get-tuple-element.39), channel_id=1, source_target_pairs={{0,1},{1,0},{2,3},{3,2},{4,5},{5,4},{6,7},{7,6},{8,9},{9,8},{10,11... | collective-permute-start | bytes 6782984 | tf_op jit(solution)/shard_map/ppermute | solution.py:331
  257.5 37.7 %collective-permute-start.56 = (bf16[128,2944]{1,0:T(8,128)(2,1)}, bf16[128,2944]{1,0:T(8,128)(2,1)}, u32[]{:S(2)}, u32[]{:S(2)}) collective-permute-start(bf16[128,2944]{1,0:T(8,128)(2,1)} %get-tuple-element.35), channel_id=1, source_target_pairs={{0,1},{1,0},{2,3},{3,2},{4,5},{5,4},{6,7},{7,6},{8,9},{9,8},{10,11... | collective-permute-start | bytes 2261000 | tf_op jit(solution)/shard_map/ppermute | solution.py:331
  262.0 33.3 %collective-permute-start.49 = (bf16[64,2944]{1,0:T(8,128)(2,1)}, bf16[64,2944]{1,0:T(8,128)(2,1)}, u32[]{:S(2)}, u32[]{:S(2)}) collective-permute-start(bf16[64,2944]{1,0:T(8,128)(2,1)} %slice.274), channel_id=1, source_target_pairs={{0,16},{16,0},{1,17},{17,1},{2,18},{18,2},{3,19},{19,3},{4,20},{20... | collective-permute-start | bytes 1130504 | tf_op jit(solution)/shard_map/ppermute | solution.py:331
  263.4 32.4 %collective-permute-start.50 = (bf16[64,2944]{1,0:T(8,128)(2,1)}, bf16[64,2944]{1,0:T(8,128)(2,1)}, u32[]{:S(2)}, u32[]{:S(2)}) collective-permute-start(bf16[64,2944]{1,0:T(8,128)(2,1)} %slice.275), channel_id=1, source_target_pairs={{0,8},{8,0},{1,9},{9,1},{2,10},{10,2},{3,11},{11,3},{4,12},{12,4},... | collective-permute-start | bytes 1130504 | tf_op jit(solution)/shard_map/ppermute | solution.py:331
  304.4 137.6 %collective-permute-start.36 = (bf16[128,2944]{1,0:T(8,128)(2,1)}, bf16[128,2944]{1,0:T(8,128)(2,1)}, u32[]{:S(2)}, u32[]{:S(2)}) collective-permute-start(bf16[128,2944]{1,0:T(8,128)(2,1)} %pad_maximum_fusion.1), channel_id=1, source_target_pairs={{0,16},{16,0},{1,17},{17,1},{2,18},{18,2},{3,19},{19,3},{4,20},{20... | collective-permute-start | bytes 2261000 | tf_op jit(solution)/shard_map/ppermute | solution.py:331
  305.7 136.3 %collective-permute-start.35 = (bf16[128,2944]{1,0:T(8,128)(2,1)}, bf16[128,2944]{1,0:T(8,128)(2,1)}, u32[]{:S(2)}, u32[]{:S(2)}) collective-permute-start(bf16[128,2944]{1,0:T(8,128)(2,1)} %pad_maximum_fusion), channel_id=1, source_target_pairs={{0,8},{8,0},{1,9},{9,1},{2,10},{10,2},{3,11},{11,3},{4,12},{12,4},... | collective-permute-start | bytes 2261000 | tf_op jit(solution)/shard_map/ppermute | solution.py:331
  307.0 35.9 %collective-permute-start.70 = (bf16[384,2944]{1,0:T(8,128)(2,1)}, bf16[384,2944]{1,0:T(8,128)(2,1)}, u32[]{:S(2)}, u32[]{:S(2)}) collective-permute-start(bf16[384,2944]{1,0:T(8,128)(2,1)} %get-tuple-element.43), channel_id=1, source_target_pairs={{0,1},{1,0},{2,3},{3,2},{4,5},{5,4},{6,7},{7,6},{8,9},{9,8},{10,11... | collective-permute-start | bytes 6782984 | tf_op jit(solution)/shard_map/ppermute | solution.py:331
  310.3 31.2 %collective-permute-start.71 = (bf16[128,2944]{1,0:T(8,128)(2,1)}, bf16[128,2944]{1,0:T(8,128)(2,1)}, u32[]{:S(2)}, u32[]{:S(2)}) collective-permute-start(bf16[128,2944]{1,0:T(8,128)(2,1)} %get-tuple-element.44), channel_id=1, source_target_pairs={{0,1},{1,0},{2,3},{3,2},{4,5},{5,4},{6,7},{7,6},{8,9},{9,8},{10,11... | collective-permute-start | bytes 2261000 | tf_op jit(solution)/shard_map/ppermute | solution.py:331
  338.8 35.4 %collective-permute-start.59 = (bf16[384,2944]{1,0:T(8,128)(2,1)}, bf16[384,2944]{1,0:T(8,128)(2,1)S(1)}, u32[]{:S(2)}, u32[]{:S(2)}) collective-permute-start(bf16[384,2944]{1,0:T(8,128)(2,1)} %get-tuple-element.37), channel_id=1, source_target_pairs={{0,1},{1,0},{2,3},{3,2},{4,5},{5,4},{6,7},{7,6},{8,9},{9,8},{10,11... | collective-permute-start | bytes 6782984 | tf_op jit(solution)/shard_map/ppermute | solution.py:331
  341.6 19.3 %collective-permute-start.68 = (bf16[128,2944]{1,0:T(8,128)(2,1)S(1)}, bf16[128,2944]{1,0:T(8,128)(2,1)S(1)}, u32[]{:S(2)}, u32[]{:S(2)}) collective-permute-start(bf16[128,2944]{1,0:T(8,128)(2,1)S(1)} %pad_maximum_fusion.5), channel_id=1, source_target_pairs={{0,16},{16,0},{1,17},{17,1},{2,18},{18,2},{3,19},{19,3},{4,20},{20... | collective-permute-start | bytes 2261000 | tf_op jit(solution)/shard_map/ppermute | solution.py:331
  342.9 18.9 %collective-permute-start.67 = (bf16[128,2944]{1,0:T(8,128)(2,1)S(1)}, bf16[128,2944]{1,0:T(8,128)(2,1)S(1)}, u32[]{:S(2)}, u32[]{:S(2)}) collective-permute-start(bf16[128,2944]{1,0:T(8,128)(2,1)S(1)} %pad_maximum_fusion.4), channel_id=1, source_target_pairs={{0,8},{8,0},{1,9},{9,1},{2,10},{10,2},{3,11},{11,3},{4,12},{12,4},... | collective-permute-start | bytes 2261000 | tf_op jit(solution)/shard_map/ppermute | solution.py:331
  372.0 72.8 %collective-permute-start.69 = (bf16[128,2944]{1,0:T(8,128)(2,1)S(1)}, bf16[128,2944]{1,0:T(8,128)(2,1)S(1)}, u32[]{:S(2)}, u32[]{:S(2)}) collective-permute-start(bf16[128,2944]{1,0:T(8,128)(2,1)S(1)} %add_convert_fusion.6), channel_id=1, source_target_pairs={{0,4},{2,6},{4,0},{6,2},{1,5},{3,7},{5,1},{7,3},{8,12},{10,14},{12... | collective-permute-start | bytes 2261000 | tf_op jit(solution)/shard_map/ppermute | solution.py:331
  374.2 33.0 %collective-permute-start.75 = (bf16[128,2944]{1,0:T(8,128)(2,1)S(1)}, bf16[128,2944]{1,0:T(8,128)(2,1)S(1)}, u32[]{:S(2)}, u32[]{:S(2)}) collective-permute-start(bf16[128,2944]{1,0:T(8,128)(2,1)S(1)} %pad_maximum_fusion.7), channel_id=1, source_target_pairs={{0,16},{16,0},{1,17},{17,1},{2,18},{18,2},{3,19},{19,3},{4,20},{20... | collective-permute-start | bytes 2261000 | tf_op jit(solution)/shard_map/ppermute | solution.py:331
  406.3 17.0 %collective-permute-start.73 = (bf16[128,2944]{1,0:T(8,128)(2,1)S(1)}, bf16[128,2944]{1,0:T(8,128)(2,1)S(1)}, u32[]{:S(2)}, u32[]{:S(2)}) collective-permute-start(bf16[128,2944]{1,0:T(8,128)(2,1)S(1)} %pad_maximum_fusion.6), channel_id=1, source_target_pairs={{0,8},{8,0},{1,9},{9,1},{2,10},{10,2},{3,11},{11,3},{4,12},{12,4},... | collective-permute-start | bytes 2261000 | tf_op jit(solution)/shard_map/ppermute | solution.py:331
  407.2 18.3 %collective-permute-start.64 = (bf16[128,2944]{1,0:T(8,128)(2,1)S(1)}, bf16[128,2944]{1,0:T(8,128)(2,1)S(1)}, u32[]{:S(2)}, u32[]{:S(2)}) collective-permute-start(bf16[128,2944]{1,0:T(8,128)(2,1)S(1)} %pad_maximum_fusion.3), channel_id=1, source_target_pairs={{0,16},{16,0},{1,17},{17,1},{2,18},{18,2},{3,19},{19,3},{4,20},{20... | collective-permute-start | bytes 2261000 | tf_op jit(solution)/shard_map/ppermute | solution.py:331
  423.3 15.4 %collective-permute-start.62 = (bf16[128,2944]{1,0:T(8,128)(2,1)S(1)}, bf16[128,2944]{1,0:T(8,128)(2,1)S(1)}, u32[]{:S(2)}, u32[]{:S(2)}) collective-permute-start(bf16[128,2944]{1,0:T(8,128)(2,1)S(1)} %pad_maximum_fusion.2), channel_id=1, source_target_pairs={{0,8},{8,0},{1,9},{9,1},{2,10},{10,2},{3,11},{11,3},{4,12},{12,4},... | collective-permute-start | bytes 2261000 | tf_op jit(solution)/shard_map/ppermute | solution.py:331
  425.5 19.3 %collective-permute-start.76 = (bf16[128,2944]{1,0:T(8,128)(2,1)S(1)}, bf16[128,2944]{1,0:T(8,128)(2,1)S(1)}, u32[]{:S(2)}, u32[]{:S(2)}) collective-permute-start(bf16[128,2944]{1,0:T(8,128)(2,1)S(1)} %add_convert_fusion), channel_id=1, source_target_pairs={{0,6},{2,4},{4,2},{6,0},{1,7},{3,5},{5,3},{7,1},{8,14},{10,12},{12... | collective-permute-start | bytes 2261000 | tf_op jit(solution)/shard_map/ppermute | solution.py:331
  439.1 18.8 %collective-permute-start.65 = (bf16[128,2944]{1,0:T(8,128)(2,1)S(1)}, bf16[128,2944]{1,0:T(8,128)(2,1)S(1)}, u32[]{:S(2)}, u32[]{:S(2)}) collective-permute-start(bf16[128,2944]{1,0:T(8,128)(2,1)S(1)} %add_convert_fusion.11), channel_id=1, source_target_pairs={{0,2},{2,0},{4,6},{6,4},{1,3},{3,1},{5,7},{7,5},{8,10},{10,8},{12,... | collective-permute-start | bytes 2261000 | tf_op jit(solution)/shard_map/ppermute | solution.py:331
  (83 other events, 858.5 us)
